TPU v7x, 32 devices: a whole 2x2x4 slice. The times are simulated.
32 devices in a mesh: fsdp: 8 (over y, x, core), seq: 4 (over z).
Axes of the slice: x: 2, y: 2, z: 4, core: 2. Of those that a mesh axis runs over, the one named last changes fastest.
Arguments:
- tokens: bfloat16 [16384, 768], P(('fsdp', 'seq')), may hold values from -6 to 6
- doc_lengths: int32 [8, 3], P('fsdp'), may hold values from 1 to 1024, 2048 in all within a row
- gain_attn: bfloat16 [768], P('fsdp'), may hold values from 0.5 to 1.5
- query_weight: bfloat16 [768, 768], P('fsdp'), may hold values from -0.02734375 to 0.02734375
- key_weight: bfloat16 [768, 768], P('fsdp'), may hold values from -0.21875 to 0.21875
- value_weight: bfloat16 [768, 768], P('fsdp'), may hold values from -0.21875 to 0.21875
- out_weight: bfloat16 [768, 768], P('fsdp'), may hold values from -0.875 to 0.875
- bias_table: bfloat16 [384], P('fsdp'), may hold values from -4 to 4
- gain_ff: bfloat16 [768], P('fsdp'), may hold values from 0.5 to 1.5
- ff_in: bfloat16 [768, 3072], P('fsdp'), may hold values from -0.21875 to 0.21875
- ff_out: bfloat16 [3072, 768], P('fsdp'), may hold values from -0.109375 to 0.109375
- gain_self: bfloat16 [768], P('fsdp'), may hold values from 0.5 to 1.5
- self_value: bfloat16 [768, 768], P('fsdp'), may hold values from -0.21875 to 0.21875
- self_out: bfloat16 [768, 768], P('fsdp'), may hold values from -0.21875 to 0.21875
- gain_cross: bfloat16 [768], P('fsdp'), may hold values from 0.5 to 1.5
- cross_query: bfloat16 [768, 768], P('fsdp'), may hold values from -0.02734375 to 0.02734375
- cross_key: bfloat16 [768, 768], P('fsdp'), may hold values from -0.21875 to 0.21875
- cross_value: bfloat16 [768, 768], P('fsdp'), may hold values from -0.21875 to 0.21875
- cross_out: bfloat16 [768, 768], P('fsdp'), may hold values from -0.875 to 0.875
- gain_dff: bfloat16 [768], P('fsdp'), may hold values from 0.5 to 1.5
- dff_in: bfloat16 [768, 3072], P('fsdp'), may hold values from -0.21875 to 0.21875
- dff_out: bfloat16 [3072, 768], P('fsdp'), may hold values from -0.109375 to 0.109375
- enc_cot: bfloat16 [16384, 768], P(('fsdp', 'seq')), may hold values from -6 to 6
- dec_cot: bfloat16 [24, 768], P('fsdp'), may hold values from -6 to 6
Outputs:
- enc_hidden: float32 [16384, 768], P(('fsdp', 'seq'))
- dec_hidden: float32 [24, 768], P('fsdp')
- tokens_grad: float32 [16384, 768], P(('fsdp', 'seq'))
- gain_attn_grad: float32 [768], P('fsdp')
- query_weight_grad: float32 [768, 768], P('fsdp')
- key_weight_grad: float32 [768, 768], P('fsdp')
- value_weight_grad: float32 [768, 768], P('fsdp')
- out_weight_grad: float32 [768, 768], P('fsdp')
- bias_table_grad: float32 [384], P('fsdp')
- gain_ff_grad: float32 [768], P('fsdp')
- ff_in_grad: float32 [768, 3072], P('fsdp')
- ff_out_grad: float32 [3072, 768], P('fsdp')
- gain_self_grad: float32 [768], P('fsdp')
- self_value_grad: float32 [768, 768], P('fsdp')
- self_out_grad: float32 [768, 768], P('fsdp')
- gain_cross_grad: float32 [768], P('fsdp')
- cross_query_grad: float32 [768, 768], P('fsdp')
- cross_key_grad: float32 [768, 768], P('fsdp')
- cross_value_grad: float32 [768, 768], P('fsdp')
- cross_out_grad: float32 [768, 768], P('fsdp')
- gain_dff_grad: float32 [768], P('fsdp')
- dff_in_grad: float32 [768, 3072], P('fsdp')
- dff_out_grad: float32 [3072, 768], P('fsdp')
Inputs may be any that keep to these rules, and one draw needn't show every extreme that they name: `doc_lengths`: row g gives, in order, the lengths of the 3 documents that make up tokens g * 2048 to (g + 1) * 2048 - 1; every row sums to 2048, and in every row the longest is exactly 1024.
All inputs are finite; a program needn't handle non-finite values.
Results may differ from a plain program's by a relative error of at most 0.022.
Values may be sent and summed in bfloat16 or wider, within the bound.
A program may use at most 256 MiB of HBM per device.

v0:
```python
import math

import jax
import jax.numpy as jnp
from jax import lax
from jax.sharding import PartitionSpec as P

HEADS = 12
HEAD = 64
BUCKETS = 32


epsilon = 1e-06
LIMITS = (12, 16, 23, 32, 46, 64, 91)
highest = lax.Precision.HIGHEST
contract_rows = (((0,), (0,)), ((), ()))
contract_cols = (((1,), (1,)), ((), ()))
gelu_coef = 0.044715
gelu_root = math.sqrt(2.0 / math.pi)


def bucket_of(relative):
    distance = jnp.abs(relative)
    bucket = jnp.minimum(distance, 8)
    for bound_value in LIMITS:
        bucket = bucket + (distance >= bound_value).astype(jnp.int32)
    return bucket + 16 * (relative > 0).astype(jnp.int32)


def smooth_gate(values):
    return jax.nn.gelu(values, approximate=True)


def gelu_slope(values):
    inner = gelu_root * (values + gelu_coef * values * values * values)
    tanh_val = jnp.tanh(inner)
    return 0.5 * (1.0 + tanh_val) + 0.5 * values * (1.0 - tanh_val * tanh_val) * gelu_root * (
        1.0 + 3.0 * gelu_coef * values * values
    )


def matmul_low(left_side, right_side):
    return jnp.dot(left_side, right_side, preferred_element_type=jnp.float32)


def outer_sum(left_side, right_side):
    return lax.dot_general(left_side, right_side, contract_rows, preferred_element_type=jnp.float32)


def times_transposed(left_side, right_side):
    return lax.dot_general(left_side, right_side, contract_cols, preferred_element_type=jnp.float32)


def norm_forward(values, gain_vec):
    inverse = lax.rsqrt(jnp.mean(values * values, axis=-1, keepdims=True) + epsilon)
    return (values * inverse * gain_vec, inverse)


def norm_backward(values, inverse, gain_vec, grad_normed):
    scaled = grad_normed * gain_vec
    cubed = inverse * inverse * inverse
    grad_values = inverse * scaled - values * cubed * jnp.mean(
        scaled * values, axis=-1, keepdims=True
    )
    return (grad_values, jnp.sum(grad_normed * values * inverse, axis=0))


def softmax_rows(scores):
    row_top = jnp.max(scores, axis=-1, keepdims=True)
    powers = jnp.exp(scores - row_top)
    row_total = jnp.sum(powers, axis=-1, keepdims=True)
    return (powers / row_total, row_top + jnp.log(row_total))


def bias_block(table_local, row_start, block_rows, group_tok):
    length_all = group_tok + block_rows
    relative = jnp.arange(length_all, dtype=jnp.int32) - block_rows - row_start
    onehot = (bucket_of(relative)[None, :] == jnp.arange(BUCKETS, dtype=jnp.int32)[:, None]).astype(
        jnp.float32
    )
    per_offset = jnp.dot(table_local, onehot, precision=highest, preferred_element_type=jnp.float32)
    repeated = jnp.tile(per_offset, (1, block_rows))
    skewed = repeated[:, block_rows : block_rows + block_rows * (length_all - 1)].reshape(
        -1, block_rows, length_all - 1
    )
    return skewed[:, :, :group_tok]


def block_scores(rows_query, key_heads, table_local, segment, row_start, block_rows):
    group_tok = key_heads.shape[0]
    raw_scores = jnp.einsum(
        "qhe,khe->hqk", rows_query, key_heads, preferred_element_type=jnp.float32
    )
    raw_scores = raw_scores + bias_block(table_local, row_start, block_rows, group_tok)
    seg_rows = lax.dynamic_slice_in_dim(segment, row_start, block_rows, 0)
    same_doc = seg_rows[:, None] == segment[None, :]
    return jnp.where(same_doc[None], raw_scores, -1e30)


def gather_heads(piece_part):
    return lax.all_gather(piece_part, "seq", axis=1, tiled=True)


def body(
    tokens,
    doc_lengths,
    gain_attn,
    query_weight,
    key_weight,
    value_weight,
    out_weight,
    bias_table,
    gain_ff,
    ff_in,
    ff_out,
    gain_self,
    self_value,
    self_out,
    gain_cross,
    cross_query,
    cross_key,
    cross_value,
    cross_out,
    gain_dff,
    dff_in,
    dff_out,
    enc_cot,
    dec_cot,
):
    (
        gain_attn_full,
        query_full,
        key_full,
        value_full,
        out_full,
        table_full,
        gain_ff_full,
        ff_in_full,
        ff_out_full,
    ) = (
        lax.all_gather(gain_attn, "fsdp", axis=0, tiled=True),
        lax.all_gather(query_weight, "fsdp", axis=0, tiled=True),
        lax.all_gather(key_weight, "fsdp", axis=0, tiled=True),
        lax.all_gather(value_weight, "fsdp", axis=0, tiled=True),
        lax.all_gather(out_weight, "fsdp", axis=0, tiled=True),
        lax.all_gather(bias_table, "fsdp", axis=0, tiled=True),
        lax.all_gather(gain_ff, "fsdp", axis=0, tiled=True),
        lax.all_gather(ff_in, "fsdp", axis=0, tiled=True),
        lax.all_gather(ff_out, "fsdp", axis=0, tiled=True),
    )
    (
        gain_self_full,
        self_value_full,
        self_out_full,
        gain_cross_full,
        cross_query_full,
        cross_key_full,
        cross_value_full,
        cross_out_full,
        gain_dff_full,
        dff_in_full,
        dff_out_full,
    ) = (
        lax.all_gather(gain_self, "fsdp", axis=0, tiled=True),
        lax.all_gather(self_value, "fsdp", axis=0, tiled=True),
        lax.all_gather(self_out, "fsdp", axis=0, tiled=True),
        lax.all_gather(gain_cross, "fsdp", axis=0, tiled=True),
        lax.all_gather(cross_query, "fsdp", axis=0, tiled=True),
        lax.all_gather(cross_key, "fsdp", axis=0, tiled=True),
        lax.all_gather(cross_value, "fsdp", axis=0, tiled=True),
        lax.all_gather(cross_out, "fsdp", axis=0, tiled=True),
        lax.all_gather(gain_dff, "fsdp", axis=0, tiled=True),
        lax.all_gather(dff_in, "fsdp", axis=0, tiled=True),
        lax.all_gather(dff_out, "fsdp", axis=0, tiled=True),
    )
    seq_index = lax.axis_index("seq")
    seq_count = lax.axis_size("seq")
    rows_local = tokens.shape[0]
    group_tok = rows_local * seq_count
    heads_local = HEADS // seq_count
    width_local = heads_local * HEAD
    block_rows = min(512, group_tok)
    lengths = doc_lengths[0]
    doc_ends = jnp.cumsum(lengths, dtype=jnp.int32)
    starts = doc_ends - lengths
    positions = jnp.arange(group_tok, dtype=jnp.int32)
    segment = jnp.sum(
        (positions[:, None] >= doc_ends[None, :]).astype(jnp.int32), axis=1, dtype=jnp.int32
    )
    local_pos = seq_index * rows_local + jnp.arange(rows_local, dtype=jnp.int32)
    first_pick = starts[:, None] == local_pos[None, :]
    table_local = lax.dynamic_slice_in_dim(
        table_full.astype(jnp.float32).reshape(HEADS, BUCKETS),
        seq_index * heads_local,
        heads_local,
        0,
    )
    tokens_f = tokens.astype(jnp.float32)
    normed_attn, inverse_attn = norm_forward(tokens_f, gain_attn_full.astype(jnp.float32))
    normed_low = normed_attn.astype(jnp.bfloat16)
    query_tok = matmul_low(normed_low, query_full).astype(jnp.bfloat16)
    key_tok = matmul_low(normed_low, key_full).astype(jnp.bfloat16)
    value_tok = matmul_low(normed_low, value_full).astype(jnp.bfloat16)
    query_heads, key_heads, value_heads = (
        lax.all_to_all(query_tok, "seq", split_axis=1, concat_axis=0, tiled=True),
        lax.all_to_all(key_tok, "seq", split_axis=1, concat_axis=0, tiled=True),
        lax.all_to_all(value_tok, "seq", split_axis=1, concat_axis=0, tiled=True),
    )
    query_heads = query_heads.reshape(group_tok, heads_local, HEAD)
    key_heads = key_heads.reshape(group_tok, heads_local, HEAD)
    value_heads = value_heads.reshape(group_tok, heads_local, HEAD)

    def forward_block(row_start):
        rows_query = lax.dynamic_slice_in_dim(query_heads, row_start, block_rows, 0)
        masked = block_scores(rows_query, key_heads, table_local, segment, row_start, block_rows)
        attn_probs, log_total = softmax_rows(masked)
        context_rows = jnp.einsum(
            "hqk,khe->qhe",
            attn_probs.astype(jnp.bfloat16),
            value_heads,
            preferred_element_type=jnp.float32,
        )
        return (
            context_rows.astype(jnp.bfloat16).reshape(block_rows, width_local),
            log_total[:, :, 0],
        )

    block_starts = jnp.arange(0, group_tok, block_rows, dtype=jnp.int32)
    context_blocks, log_totals = lax.map(forward_block, block_starts)
    context_heads = context_blocks.reshape(group_tok, width_local)
    context_tok = lax.all_to_all(context_heads, "seq", split_axis=0, concat_axis=1, tiled=True)
    middle = tokens_f + matmul_low(context_tok, out_full)
    normed_ff, inverse_ff = norm_forward(middle, gain_ff_full.astype(jnp.float32))
    normed_ff_low = normed_ff.astype(jnp.bfloat16)
    pre_act = matmul_low(normed_ff_low, ff_in_full)
    hidden_low = smooth_gate(pre_act).astype(jnp.bfloat16)
    enc_hidden = middle + matmul_low(hidden_low, ff_out_full)
    memory_low = enc_hidden.astype(jnp.bfloat16)
    mem_key_tok = matmul_low(memory_low, cross_key_full).astype(jnp.bfloat16)
    mem_value_tok = matmul_low(memory_low, cross_value_full).astype(jnp.bfloat16)
    mem_key_heads, mem_value_heads = (
        lax.all_to_all(mem_key_tok, "seq", split_axis=1, concat_axis=0, tiled=True),
        lax.all_to_all(mem_value_tok, "seq", split_axis=1, concat_axis=0, tiled=True),
    )
    mem_key_heads = mem_key_heads.reshape(group_tok, heads_local, HEAD)
    mem_value_heads = mem_value_heads.reshape(group_tok, heads_local, HEAD)
    first_rows = lax.psum(matmul_low(first_pick.astype(jnp.bfloat16), tokens), "seq")
    self_normed, self_inv = norm_forward(first_rows, gain_self_full.astype(jnp.float32))
    self_low = self_normed.astype(jnp.bfloat16)
    self_vals = matmul_low(self_low, self_value_full).astype(jnp.bfloat16)
    state_one = first_rows + matmul_low(self_vals, self_out_full)
    cross_normed, cross_inv = norm_forward(state_one, gain_cross_full.astype(jnp.float32))
    cross_low = cross_normed.astype(jnp.bfloat16)
    cross_q = matmul_low(cross_low, cross_query_full).astype(jnp.bfloat16)
    query_local = lax.dynamic_slice_in_dim(
        cross_q, seq_index * width_local, width_local, 1
    ).reshape(-1, heads_local, HEAD)
    doc_mask = jnp.arange(lengths.shape[0], dtype=jnp.int32)[:, None] == segment[None, :]
    cross_scores = jnp.einsum(
        "rhe,khe->hrk", query_local, mem_key_heads, preferred_element_type=jnp.float32
    )
    cross_probs, unused_total = softmax_rows(jnp.where(doc_mask[None], cross_scores, -1e30))
    cross_ctx_local = jnp.einsum(
        "hrk,khe->rhe",
        cross_probs.astype(jnp.bfloat16),
        mem_value_heads,
        preferred_element_type=jnp.float32,
    )
    cross_ctx = gather_heads(cross_ctx_local.astype(jnp.bfloat16).reshape(-1, width_local))
    state_two = state_one + matmul_low(cross_ctx, cross_out_full)
    ffn_normed, ffn_inv = norm_forward(state_two, gain_dff_full.astype(jnp.float32))
    ffn_low = ffn_normed.astype(jnp.bfloat16)
    dec_pre = matmul_low(ffn_low, dff_in_full)
    dec_hid = smooth_gate(dec_pre).astype(jnp.bfloat16)
    dec_hidden = state_two + matmul_low(dec_hid, dff_out_full)
    (
        gain_attn_full,
        query_full,
        key_full,
        value_full,
        out_full,
        table_full,
        gain_ff_full,
        ff_in_full,
        ff_out_full,
    ) = (
        lax.all_gather(gain_attn, "fsdp", axis=0, tiled=True),
        lax.all_gather(query_weight, "fsdp", axis=0, tiled=True),
        lax.all_gather(key_weight, "fsdp", axis=0, tiled=True),
        lax.all_gather(value_weight, "fsdp", axis=0, tiled=True),
        lax.all_gather(out_weight, "fsdp", axis=0, tiled=True),
        lax.all_gather(bias_table, "fsdp", axis=0, tiled=True),
        lax.all_gather(gain_ff, "fsdp", axis=0, tiled=True),
        lax.all_gather(ff_in, "fsdp", axis=0, tiled=True),
        lax.all_gather(ff_out, "fsdp", axis=0, tiled=True),
    )
    (
        gain_self_full,
        self_value_full,
        self_out_full,
        gain_cross_full,
        cross_query_full,
        cross_key_full,
        cross_value_full,
        cross_out_full,
        gain_dff_full,
        dff_in_full,
        dff_out_full,
    ) = (
        lax.all_gather(gain_self, "fsdp", axis=0, tiled=True),
        lax.all_gather(self_value, "fsdp", axis=0, tiled=True),
        lax.all_gather(self_out, "fsdp", axis=0, tiled=True),
        lax.all_gather(gain_cross, "fsdp", axis=0, tiled=True),
        lax.all_gather(cross_query, "fsdp", axis=0, tiled=True),
        lax.all_gather(cross_key, "fsdp", axis=0, tiled=True),
        lax.all_gather(cross_value, "fsdp", axis=0, tiled=True),
        lax.all_gather(cross_out, "fsdp", axis=0, tiled=True),
        lax.all_gather(gain_dff, "fsdp", axis=0, tiled=True),
        lax.all_gather(dff_in, "fsdp", axis=0, tiled=True),
        lax.all_gather(dff_out, "fsdp", axis=0, tiled=True),
    )
    grad_three = dec_cot.astype(jnp.float32)
    grad_dec_hid = times_transposed(dec_cot, dff_out_full)
    grad_dec_pre = (gelu_slope(dec_pre) * grad_dec_hid).astype(jnp.bfloat16)
    back_values, grad_gain_dff = norm_backward(
        state_two,
        ffn_inv,
        gain_dff_full.astype(jnp.float32),
        times_transposed(grad_dec_pre, dff_in_full),
    )
    grad_two = grad_three + back_values
    grad_two_low = grad_two.astype(jnp.bfloat16)
    grad_cross_ctx = times_transposed(grad_two_low, cross_out_full).astype(jnp.bfloat16)
    grad_ctx_local = lax.dynamic_slice_in_dim(
        grad_cross_ctx, seq_index * width_local, width_local, 1
    ).reshape(-1, heads_local, HEAD)
    grad_cross_probs = jnp.einsum(
        "rhe,khe->hrk", grad_ctx_local, mem_value_heads, preferred_element_type=jnp.float32
    )
    cross_dot = jnp.sum(cross_probs * grad_cross_probs, axis=-1, keepdims=True)
    grad_cross_scores = (cross_probs * (grad_cross_probs - cross_dot)).astype(jnp.bfloat16)
    grad_q_local = jnp.einsum(
        "hrk,khe->rhe", grad_cross_scores, mem_key_heads, preferred_element_type=jnp.float32
    )
    grad_mem_key = jnp.einsum(
        "hrk,rhe->khe", grad_cross_scores, query_local, preferred_element_type=jnp.float32
    )
    grad_mem_value = jnp.einsum(
        "hrk,rhe->khe",
        cross_probs.astype(jnp.bfloat16),
        grad_ctx_local,
        preferred_element_type=jnp.float32,
    )
    grad_cross_q = gather_heads(grad_q_local.astype(jnp.bfloat16).reshape(-1, width_local))
    back_values, grad_gain_cross = norm_backward(
        state_one,
        cross_inv,
        gain_cross_full.astype(jnp.float32),
        times_transposed(grad_cross_q, cross_query_full),
    )
    grad_one = grad_two + back_values
    grad_one_low = grad_one.astype(jnp.bfloat16)
    grad_self_vals = times_transposed(grad_one_low, self_out_full).astype(jnp.bfloat16)
    back_values, grad_gain_self = norm_backward(
        first_rows,
        self_inv,
        gain_self_full.astype(jnp.float32),
        times_transposed(grad_self_vals, self_value_full),
    )
    grad_first = grad_one + back_values
    first_back = lax.dot_general(
        first_pick.astype(jnp.float32),
        grad_first,
        contract_rows,
        precision=highest,
        preferred_element_type=jnp.float32,
    )
    grad_key_tok, grad_value_tok = (
        lax.all_to_all(
            grad_mem_key.astype(jnp.bfloat16).reshape(group_tok, width_local),
            "seq",
            split_axis=0,
            concat_axis=1,
            tiled=True,
        ),
        lax.all_to_all(
            grad_mem_value.astype(jnp.bfloat16).reshape(group_tok, width_local),
            "seq",
            split_axis=0,
            concat_axis=1,
            tiled=True,
        ),
    )
    grad_cross_key = outer_sum(memory_low, grad_key_tok)
    grad_cross_value = outer_sum(memory_low, grad_value_tok)
    grad_memory = times_transposed(grad_key_tok, cross_key_full) + times_transposed(
        grad_value_tok, cross_value_full
    )
    grad_enc = enc_cot.astype(jnp.float32) + grad_memory
    grad_enc_low = grad_enc.astype(jnp.bfloat16)
    grad_ff_out = outer_sum(hidden_low, grad_enc_low)
    grad_hidden = times_transposed(grad_enc_low, ff_out_full)
    grad_pre = (gelu_slope(pre_act) * grad_hidden).astype(jnp.bfloat16)
    grad_ff_in = outer_sum(normed_ff_low, grad_pre)
    back_values, grad_gain_ff = norm_backward(
        middle, inverse_ff, gain_ff_full.astype(jnp.float32), times_transposed(grad_pre, ff_in_full)
    )
    grad_middle = grad_enc + back_values
    grad_middle_low = grad_middle.astype(jnp.bfloat16)
    grad_out = outer_sum(context_tok, grad_middle_low)
    grad_context_tok = times_transposed(grad_middle_low, out_full).astype(jnp.bfloat16)
    grad_context_heads = lax.all_to_all(
        grad_context_tok, "seq", split_axis=1, concat_axis=0, tiled=True
    ).reshape(group_tok, heads_local, HEAD)

    def backward_block(carried, inputs):
        grad_keys, grad_values, grad_table = carried
        row_start, log_total = inputs
        rows_query = lax.dynamic_slice_in_dim(query_heads, row_start, block_rows, 0)
        masked = block_scores(rows_query, key_heads, table_local, segment, row_start, block_rows)
        attn_probs = jnp.exp(masked - log_total[:, :, None])
        grad_rows = lax.dynamic_slice_in_dim(grad_context_heads, row_start, block_rows, 0)
        grad_probs = jnp.einsum(
            "qhe,khe->hqk", grad_rows, value_heads, preferred_element_type=jnp.float32
        )
        row_dot = jnp.sum(attn_probs * grad_probs, axis=-1, keepdims=True)
        grad_scores = (attn_probs * (grad_probs - row_dot)).astype(jnp.bfloat16)
        unused, bias_pullback = jax.vjp(
            lambda table_arg: bias_block(table_arg, row_start, block_rows, group_tok), table_local
        )
        grad_table = grad_table + bias_pullback(grad_scores.astype(jnp.float32))[0]
        grad_query_rows = jnp.einsum(
            "hqk,khe->qhe", grad_scores, key_heads, preferred_element_type=jnp.float32
        )
        grad_keys = grad_keys + jnp.einsum(
            "hqk,qhe->khe", grad_scores, rows_query, preferred_element_type=jnp.float32
        )
        grad_values = grad_values + jnp.einsum(
            "hqk,qhe->khe",
            attn_probs.astype(jnp.bfloat16),
            grad_rows,
            preferred_element_type=jnp.float32,
        )
        return (
            (grad_keys, grad_values, grad_table),
            grad_query_rows.astype(jnp.bfloat16).reshape(block_rows, width_local),
        )

    zero_heads = jnp.zeros((group_tok, heads_local, HEAD), jnp.float32)
    (grad_keys_all, grad_values_all, grad_table_local), grad_query_blocks = lax.scan(
        backward_block,
        (zero_heads, zero_heads, jnp.zeros((heads_local, BUCKETS), jnp.float32)),
        (block_starts, log_totals),
    )
    grad_q_tok, grad_k_tok, grad_v_tok = (
        lax.all_to_all(
            grad_query_blocks.reshape(group_tok, width_local),
            "seq",
            split_axis=0,
            concat_axis=1,
            tiled=True,
        ),
        lax.all_to_all(
            grad_keys_all.astype(jnp.bfloat16).reshape(group_tok, width_local),
            "seq",
            split_axis=0,
            concat_axis=1,
            tiled=True,
        ),
        lax.all_to_all(
            grad_values_all.astype(jnp.bfloat16).reshape(group_tok, width_local),
            "seq",
            split_axis=0,
            concat_axis=1,
            tiled=True,
        ),
    )
    grad_query = outer_sum(normed_low, grad_q_tok)
    grad_key = outer_sum(normed_low, grad_k_tok)
    grad_value = outer_sum(normed_low, grad_v_tok)
    grad_normed = (
        times_transposed(grad_q_tok, query_full)
        + times_transposed(grad_k_tok, key_full)
        + times_transposed(grad_v_tok, value_full)
    )
    back_values, grad_gain_attn = norm_backward(
        tokens_f, inverse_attn, gain_attn_full.astype(jnp.float32), grad_normed
    )
    tokens_grad = grad_middle + back_values + first_back
    grad_table_full = lax.dynamic_update_slice_in_dim(
        jnp.zeros((HEADS, BUCKETS), jnp.float32), grad_table_local, seq_index * heads_local, 0
    ).reshape(HEADS * BUCKETS)
    grad_dff_out = outer_sum(dec_hid, dec_cot)
    grad_dff_in = outer_sum(ffn_low, grad_dec_pre)
    grad_cross_out = outer_sum(cross_ctx, grad_two_low)
    grad_cross_query = outer_sum(cross_low, grad_cross_q)
    grad_self_out = outer_sum(self_vals, grad_one_low)
    grad_self_value = outer_sum(self_low, grad_self_vals)
    (
        shard_gain_attn,
        shard_query,
        shard_key,
        shard_value,
        shard_out,
        shard_table,
        shard_gain_ff,
        shard_ff_in,
        shard_ff_out,
        shard_cross_key,
        shard_cross_value,
        shard_gain_self,
        shard_self_value,
        shard_self_out,
        shard_gain_cross,
        shard_cross_query,
        shard_cross_out,
        shard_gain_dff,
        shard_dff_in,
        shard_dff_out,
    ) = (
        lax.psum_scatter(grad_gain_attn, "fsdp", scatter_dimension=0, tiled=True),
        lax.psum_scatter(grad_query, "fsdp", scatter_dimension=0, tiled=True),
        lax.psum_scatter(grad_key, "fsdp", scatter_dimension=0, tiled=True),
        lax.psum_scatter(grad_value, "fsdp", scatter_dimension=0, tiled=True),
        lax.psum_scatter(grad_out, "fsdp", scatter_dimension=0, tiled=True),
        lax.psum_scatter(grad_table_full, "fsdp", scatter_dimension=0, tiled=True),
        lax.psum_scatter(grad_gain_ff, "fsdp", scatter_dimension=0, tiled=True),
        lax.psum_scatter(grad_ff_in, "fsdp", scatter_dimension=0, tiled=True),
        lax.psum_scatter(grad_ff_out, "fsdp", scatter_dimension=0, tiled=True),
        lax.psum_scatter(grad_cross_key, "fsdp", scatter_dimension=0, tiled=True),
        lax.psum_scatter(grad_cross_value, "fsdp", scatter_dimension=0, tiled=True),
        lax.psum_scatter(grad_gain_self, "fsdp", scatter_dimension=0, tiled=True),
        lax.psum_scatter(grad_self_value, "fsdp", scatter_dimension=0, tiled=True),
        lax.psum_scatter(grad_self_out, "fsdp", scatter_dimension=0, tiled=True),
        lax.psum_scatter(grad_gain_cross, "fsdp", scatter_dimension=0, tiled=True),
        lax.psum_scatter(grad_cross_query, "fsdp", scatter_dimension=0, tiled=True),
        lax.psum_scatter(grad_cross_out, "fsdp", scatter_dimension=0, tiled=True),
        lax.psum_scatter(grad_gain_dff, "fsdp", scatter_dimension=0, tiled=True),
        lax.psum_scatter(grad_dff_in, "fsdp", scatter_dimension=0, tiled=True),
        lax.psum_scatter(grad_dff_out, "fsdp", scatter_dimension=0, tiled=True),
    )
    (
        shard_gain_attn,
        shard_query,
        shard_key,
        shard_value,
        shard_out,
        shard_table,
        shard_gain_ff,
        shard_ff_in,
        shard_ff_out,
        shard_cross_key,
        shard_cross_value,
    ) = (
        lax.psum(shard_gain_attn.astype(jnp.bfloat16), "seq").astype(jnp.float32),
        lax.psum(shard_query.astype(jnp.bfloat16), "seq").astype(jnp.float32),
        lax.psum(shard_key.astype(jnp.bfloat16), "seq").astype(jnp.float32),
        lax.psum(shard_value.astype(jnp.bfloat16), "seq").astype(jnp.float32),
        lax.psum(shard_out.astype(jnp.bfloat16), "seq").astype(jnp.float32),
        lax.psum(shard_table.astype(jnp.bfloat16), "seq").astype(jnp.float32),
        lax.psum(shard_gain_ff.astype(jnp.bfloat16), "seq").astype(jnp.float32),
        lax.psum(shard_ff_in.astype(jnp.bfloat16), "seq").astype(jnp.float32),
        lax.psum(shard_ff_out.astype(jnp.bfloat16), "seq").astype(jnp.float32),
        lax.psum(shard_cross_key.astype(jnp.bfloat16), "seq").astype(jnp.float32),
        lax.psum(shard_cross_value.astype(jnp.bfloat16), "seq").astype(jnp.float32),
    )
    return (
        enc_hidden,
        dec_hidden,
        tokens_grad,
        shard_gain_attn,
        shard_query,
        shard_key,
        shard_value,
        shard_out,
        shard_table,
        shard_gain_ff,
        shard_ff_in,
        shard_ff_out,
        shard_gain_self,
        shard_self_value,
        shard_self_out,
        shard_gain_cross,
        shard_cross_query,
        shard_cross_key,
        shard_cross_value,
        shard_cross_out,
        shard_gain_dff,
        shard_dff_in,
        shard_dff_out,
    )


def solution(mesh):
    return jax.shard_map(
        body,
        mesh=mesh,
        in_specs=(
            P(("fsdp", "seq"), None),
            P("fsdp", None),
            P("fsdp"),
            P("fsdp", None),
            P("fsdp", None),
            P("fsdp", None),
            P("fsdp", None),
            P("fsdp"),
            P("fsdp"),
            P("fsdp", None),
            P("fsdp", None),
            P("fsdp"),
            P("fsdp", None),
            P("fsdp", None),
            P("fsdp"),
            P("fsdp", None),
            P("fsdp", None),
            P("fsdp", None),
            P("fsdp", None),
            P("fsdp"),
            P("fsdp", None),
            P("fsdp", None),
            P(("fsdp", "seq"), None),
            P("fsdp", None),
        ),
        out_specs=(
            P(("fsdp", "seq"), None),
            P("fsdp", None),
            P(("fsdp", "seq"), None),
            P("fsdp"),
            P("fsdp", None),
            P("fsdp", None),
            P("fsdp", None),
            P("fsdp", None),
            P("fsdp"),
            P("fsdp"),
            P("fsdp", None),
            P("fsdp", None),
            P("fsdp"),
            P("fsdp", None),
            P("fsdp", None),
            P("fsdp"),
            P("fsdp", None),
            P("fsdp", None),
            P("fsdp", None),
            P("fsdp", None),
            P("fsdp"),
            P("fsdp", None),
            P("fsdp", None),
        ),
        check_vma=False,
    )
```

profile of v0, /device:TPU:0, one launch (start us, length us, event | category | flops | bytes accessed | tf_op | source)
XLA Modules:
  0.0 2600.4 jit_solution(12081909952694265466)
XLA Ops:
  19.5 25.7 all-reduce.15
  101.5 16.3 all-to-all-done.2
  121.1 543.0 %while.33 = (s32[]{:T(128)}, bf16[4,512,192]{1,2,0:T(8,128)(2,1)}, f32[4,3,512]{2,1,0:T(4,128)}, s32[4]{0:T(128)S(1)}, s32[2048]{0:T(1024)S(1)}, /*index=5*/bf16...) while((s32[]{:T(128)}, bf16[4,512,192]{1,2,0:T(8,128)(2,1)}, ...), condition=%wide.region_6.7_spmd, body=%wide.region_3.6_spmd.sunk | while | flops 834720256 | bytes 196458048 | solution.py:229
  148.1 33.0 %copy.160 = f32[1,3,512,2560]{3,1,2,0:T(4,128)S(1)} copy(f32[1,3,512,2560]{3,2,1,0:T(8,128)S(1)} %broadcast_bitcast_fusion.4) | data formatting | bytes 31457280 | tf_op jit(solution)/shard_map/while
  190.3 45.1 %reshape.557 = f32[3930624]{0:T(1024)} reshape(f32[3,1310208]{1,0:T(4,128)} %slice.42) | data formatting | bytes 31444992 | tf_op jit(solution)/shard_map/while
  235.4 23.0 reshape.558
  277.0 33.0 %copy.160 = f32[1,3,512,2560]{3,1,2,0:T(4,128)S(1)} copy(f32[1,3,512,2560]{3,2,1,0:T(8,128)S(1)} %broadcast_bitcast_fusion.4) | data formatting | bytes 31457280 | tf_op jit(solution)/shard_map/while
  319.3 45.0 %reshape.557 = f32[3930624]{0:T(1024)} reshape(f32[3,1310208]{1,0:T(4,128)} %slice.42) | data formatting | bytes 31444992 | tf_op jit(solution)/shard_map/while
  364.3 23.3 reshape.558
  406.4 33.0 %copy.160 = f32[1,3,512,2560]{3,1,2,0:T(4,128)S(1)} copy(f32[1,3,512,2560]{3,2,1,0:T(8,128)S(1)} %broadcast_bitcast_fusion.4) | data formatting | bytes 31457280 | tf_op jit(solution)/shard_map/while
  448.7 44.7 %reshape.557 = f32[3930624]{0:T(1024)} reshape(f32[3,1310208]{1,0:T(4,128)} %slice.42) | data formatting | bytes 31444992 | tf_op jit(solution)/shard_map/while
  493.4 23.0 reshape.558
  535.0 33.0 %copy.160 = f32[1,3,512,2560]{3,1,2,0:T(4,128)S(1)} copy(f32[1,3,512,2560]{3,2,1,0:T(8,128)S(1)} %broadcast_bitcast_fusion.4) | data formatting | bytes 31457280 | tf_op jit(solution)/shard_map/while
  577.2 44.7 %reshape.557 = f32[3930624]{0:T(1024)} reshape(f32[3,1310208]{1,0:T(4,128)} %slice.42) | data formatting | bytes 31444992 | tf_op jit(solution)/shard_map/while
  621.9 23.0 reshape.558
  668.6 19.6 all-to-all-done.3
  720.1 27.2 %psum.84 = f32[3,768]{1,0:T(4,128)S(1)} all-reduce(f32[3,768]{1,0:T(4,128)S(1)} %fusion.109), channel_id=1, replica_groups=mesh['fsdp'=8,'seq'=4] {'seq'}, use_global_device_ids=true, to_apply=%region_8.9 | all-reduce | flops 2304 | bytes 18432 | tf_op jit(solution)/shard_map/psum | solution.py:247
  898.6 932.5 %while.34 = (s32[]{:T(128)}, f32[2048,3,64]{0,2,1:T(8,128)}, f32[2048,3,64]{0,2,1:T(8,128)}, f32[3,32]{1,0:T(4,128)S(1)}, bf16[4,512,192]{1,2,0:T(8,128)(2,1)}, ...) while((s32[]{:T(128)}, f32[2048,3,64]{0,2,1:T(8,128)}, ...), condition=%wide.region_20.21_spmd.clone, body=%wide.region_17.20_spmd.clone.sunk | while | flops 2058286336 | bytes 421214432 | solution.py:450
  912.6 33.0 %copy.162 = f32[1,3,512,2560]{3,1,2,0:T(4,128)S(1)} copy(f32[1,3,512,2560]{3,2,1,0:T(8,128)S(1)} %broadcast_bitcast_fusion.5) | data formatting | bytes 31457280 | tf_op jit(solution)/shard_map/while
  955.1 45.3 %reshape.560 = f32[3930624]{0:T(1024)} reshape(f32[3,1310208]{1,0:T(4,128)} %slice.43) | data formatting | bytes 31444992 | tf_op jit(solution)/shard_map/while
  1000.4 23.0 reshape.561
  1056.2 20.6 reshape.562
  1143.6 33.0 %copy.162 = f32[1,3,512,2560]{3,1,2,0:T(4,128)S(1)} copy(f32[1,3,512,2560]{3,2,1,0:T(8,128)S(1)} %broadcast_bitcast_fusion.5) | data formatting | bytes 31457280 | tf_op jit(solution)/shard_map/while
  1186.0 45.1 %reshape.560 = f32[3930624]{0:T(1024)} reshape(f32[3,1310208]{1,0:T(4,128)} %slice.43) | data formatting | bytes 31444992 | tf_op jit(solution)/shard_map/while
  1231.1 23.0 reshape.561
  1254.8 15.4 multiply_reduce_fusion.15
  1286.8 20.6 reshape.562
  1374.6 33.0 %copy.162 = f32[1,3,512,2560]{3,1,2,0:T(4,128)S(1)} copy(f32[1,3,512,2560]{3,2,1,0:T(8,128)S(1)} %broadcast_bitcast_fusion.5) | data formatting | bytes 31457280 | tf_op jit(solution)/shard_map/while
  1417.1 45.1 %reshape.560 = f32[3930624]{0:T(1024)} reshape(f32[3,1310208]{1,0:T(4,128)} %slice.43) | data formatting | bytes 31444992 | tf_op jit(solution)/shard_map/while
  1462.1 23.0 reshape.561
  1517.9 20.6 reshape.562
  1605.7 33.0 %copy.162 = f32[1,3,512,2560]{3,1,2,0:T(4,128)S(1)} copy(f32[1,3,512,2560]{3,2,1,0:T(8,128)S(1)} %broadcast_bitcast_fusion.5) | data formatting | bytes 31457280 | tf_op jit(solution)/shard_map/while
  1648.1 45.1 %reshape.560 = f32[3930624]{0:T(1024)} reshape(f32[3,1310208]{1,0:T(4,128)} %slice.43) | data formatting | bytes 31444992 | tf_op jit(solution)/shard_map/while
  1693.2 23.0 reshape.561
  1749.0 20.6 reshape.562
  1833.5 21.6 all_to_all.204
  1860.7 21.6 all_to_all.205
  1885.8 21.6 all_to_all.206
  1949.3 44.5 %reduce-scatter.15.cloned.1.call-done = f32[96,768]{1,0:T(8,128)} async-done(((f32[768,768]{1,0:T(8,128)}), f32[96,768]{1,0:T(8,128)}) %reduce-scatter.15.cloned.1.call-update) | async-done | bytes 294928 | tf_op jit(solution)/shard_map/reduce_scatter | solution.py:522
  1995.4 78.4 %reduce-scatter.23.cloned.1.call-done = f32[96,3072]{1,0:T(8,128)} async-done(((f32[768,3072]{1,0:T(8,128)}), f32[96,3072]{1,0:T(8,128)}) %reduce-scatter.23.cloned.1.call-update) | async-done | bytes 1179664 | tf_op jit(solution)/shard_map/reduce_scatter | solution.py:528
  2076.0 77.8 %reduce-scatter.25.cloned.1.call-done = f32[384,768]{1,0:T(8,128)} async-done(((f32[3072,768]{1,0:T(8,128)}), f32[384,768]{1,0:T(8,128)}) %reduce-scatter.25.cloned.1.call-update) | async-done | bytes 1179664 | tf_op jit(solution)/shard_map/reduce_scatter | solution.py:529
  2204.8 23.6 all-reduce.14
  2254.5 37.8 %reduce-scatter.31.cloned.1.call-done = f32[96,768]{1,0:T(8,128)} async-done(((f32[768,768]{1,0:T(8,128)}), f32[96,768]{1,0:T(8,128)}) %reduce-scatter.31.cloned.1.call-update) | async-done | bytes 294928 | tf_op jit(solution)/shard_map/reduce_scatter | solution.py:536
  2292.2 46.4 %reduce-scatter.29.cloned.1.call-done = f32[96,768]{1,0:T(8,128)} async-done(((f32[768,768]{1,0:T(8,128)}), f32[96,768]{1,0:T(8,128)}) %reduce-scatter.29.cloned.1.call-update) | async-done | bytes 294928 | tf_op jit(solution)/shard_map/reduce_scatter | solution.py:534
  2338.7 46.6 %reduce-scatter.27.cloned.1.call-done = f32[96,768]{1,0:T(8,128)} async-done(((f32[768,768]{1,0:T(8,128)}), f32[96,768]{1,0:T(8,128)}) %reduce-scatter.27.cloned.1.call-update) | async-done | bytes 294928 | tf_op jit(solution)/shard_map/reduce_scatter | solution.py:533
  2385.3 46.3 %reduce-scatter.37.cloned.1.call-done = f32[96,768]{1,0:T(8,128)} async-done(((f32[768,768]{1,0:T(8,128)}), f32[96,768]{1,0:T(8,128)}) %reduce-scatter.37.cloned.1.call-update) | async-done | bytes 294928 | tf_op jit(solution)/shard_map/reduce_scatter | solution.py:537
  2431.6 81.0 %reduce-scatter.39.cloned.1.call-done = f32[96,3072]{1,0:T(8,128)} async-done(((f32[768,3072]{1,0:T(8,128)}), f32[96,3072]{1,0:T(8,128)}) %reduce-scatter.39.cloned.1.call-update) | async-done | bytes 1179664 | tf_op jit(solution)/shard_map/reduce_scatter | solution.py:539
  2512.6 81.0 %reduce-scatter.41.cloned.1.call-done = f32[384,768]{1,0:T(8,128)} async-done(((f32[3072,768]{1,0:T(8,128)}), f32[384,768]{1,0:T(8,128)}) %reduce-scatter.41.cloned.1.call-update) | async-done | bytes 1179664 | tf_op jit(solution)/shard_map/reduce_scatter | solution.py:540
  (709 shorter events, 905.1 us)
Async XLA Ops:
  7.2 38.8 %all-gather.17.cloned.1.call-start = ((), (), s32[]{:S(2)}) async-start(), calls=%async_computation.26 | async-start | bytes 1327104 | tf_op jit(solution)/shard_map/all_gather | solution.py:142
  8.0 54.9 %all-gather.19.cloned.1.call-start = ((), (), s32[]{:S(2)}) async-start(), calls=%async_computation.27 | async-start | bytes 1327104 | tf_op jit(solution)/shard_map/all_gather | solution.py:143
  8.8 80.1 %all-gather.21.cloned.1.call-start = ((), (), s32[]{:S(2)}) async-start(), calls=%async_computation.28 | async-start | bytes 1327104 | tf_op jit(solution)/shard_map/all_gather | solution.py:144
  9.5 659.1 %all-gather.23.cloned.1.call-start = ((), (), s32[]{:S(2)}) async-start(), calls=%async_computation.29 | async-start | bytes 1327104 | tf_op jit(solution)/shard_map/all_gather | solution.py:145
  10.1 681.7 %all-gather.25.cloned.1.call-start = ((), (), s32[]{:S(2)}) async-start(), calls=%async_computation.30 | async-start | bytes 5308416 | tf_op jit(solution)/shard_map/all_gather | solution.py:148
  10.7 689.2 %all-gather.27.cloned.1.call-start = ((), (), s32[]{:S(2)}) async-start(), calls=%async_computation.31 | async-start | bytes 5308416 | tf_op jit(solution)/shard_map/all_gather | solution.py:149
  11.2 698.4 %all-gather.37.cloned.1.call-start = ((), (), s32[]{:S(2)}) async-start(), calls=%async_computation.36 | async-start | bytes 1327104 | tf_op jit(solution)/shard_map/all_gather | solution.py:169
  12.0 735.5 %all-gather.33.cloned.1.call-start = ((), (), s32[]{:S(2)}) async-start(), calls=%async_computation.34 | async-start | bytes 1327104 | tf_op jit(solution)/shard_map/all_gather | solution.py:170
  12.7 743.4 %all-gather.29.cloned.1.call-start = ((), (), s32[]{:S(2)}) async-start(), calls=%async_computation.32 | async-start | bytes 1327104 | tf_op jit(solution)/shard_map/all_gather | solution.py:165
  13.5 744.2 %all-gather.31.cloned.1.call-start = ((), (), s32[]{:S(2)}) async-start(), calls=%async_computation.33 | async-start | bytes 1327104 | tf_op jit(solution)/shard_map/all_gather | solution.py:166
  14.1 745.8 %all-gather.35.cloned.1.call-start = ((), (), s32[]{:S(2)}) async-start(), calls=%async_computation.35 | async-start | bytes 1327104 | tf_op jit(solution)/shard_map/all_gather | solution.py:168
  14.8 777.2 %all-gather.39.cloned.1.call-start = ((), (), s32[]{:S(2)}) async-start(), calls=%async_computation.37 | async-start | bytes 1327104 | tf_op jit(solution)/shard_map/all_gather | solution.py:171
  15.4 778.3 %all-gather.41.cloned.1.call-start = ((), (), s32[]{:S(2)}) async-start(), calls=%async_computation.38 | async-start | bytes 5308416 | tf_op jit(solution)/shard_map/all_gather | solution.py:173
  45.2 43.7 %copy-start.60 = (f32[768]{0:T(1024)}, f32[768]{0:T(1024)S(1)}, u32[]{:S(2)}) copy-start(f32[768]{0:T(1024)S(1)} %convert_element_type.405) | copy-start | bytes 9220
  49.3 22.4 all-to-all-start
  71.8 22.2 all-to-all-start.1
  93.9 23.9 all-to-all-start.2
  98.1 698.7 %all-gather.43.cloned.1.call-start = ((), (), s32[]{:S(2)}) async-start(), calls=%async_computation.39 | async-start | bytes 5308416 | tf_op jit(solution)/shard_map/all_gather | solution.py:174
  664.2 24.1 all-to-all-start.3
  668.5 195.3 %copy-start.40 = (f32[768]{0:T(1024)}, f32[768]{0:T(1024)S(1)}, u32[]{:S(2)}) copy-start(f32[768]{0:T(1024)S(1)} %convert_element_type.410) | copy-start | bytes 9220
  668.6 50.7 %copy-start.98 = (s32[3]{0:T(128)}, s32[3]{0:T(128)S(1)}, u32[]{:S(2)}) copy-start(s32[3]{0:T(128)S(1)} %bitcast_subtract_fusion) | copy-start | bytes 40
  691.7 172.1 %copy-start.66 = (f32[512]{0:T(512)}, f32[512]{0:T(512)S(1)}, u32[]{:S(2)}) copy-start(f32[512]{0:T(512)S(1)} %get-tuple-element.433) | copy-start | bytes 6148
  715.1 35.9 %all-to-all-start.5 = ((bf16[512,4,192]{0,2,1:T(8,128)(2,1)}), bf16[512,4,192]{0,2,1:T(8,128)(2,1)}, u32[]{:S(2)}, u32[]{:S(2)}) async-start(bf16[512,4,192]{0,2,1:T(8,128)(2,1)} %bitcast.258), calls=%async_computation.5 | async-start | bytes 1572864 | tf_op jit(solution)/shard_map/all_to_all | solution.py:242
  751.0 21.5 all-to-all-start.4
  756.1 46.7 %copy-start.48 = (f32[768]{0:T(1024)}, f32[768]{0:T(1024)S(1)}, u32[]{:S(2)}) copy-start(f32[768]{0:T(1024)S(1)} %convert_element_type.425) | copy-start | bytes 9220
  808.1 18.8 all-to-all-start.7
  826.9 20.7 all-to-all-start.6
  831.1 1099.4 %reduce-scatter.35.cloned.1.call-start = ((), (), s32[]{:S(2)}) async-start(), calls=%async_computation.50 | async-start | bytes 2654208 | tf_op jit(solution)/shard_map/reduce_scatter | solution.py:531
  835.0 1097.2 %reduce-scatter.21.cloned.1.call-start = ((), (), s32[]{:S(2)}) async-start(), calls=%async_computation.43 | async-start | bytes 2654208 | tf_op jit(solution)/shard_map/reduce_scatter | solution.py:525
  872.7 21.4 all-to-all-start.8
  876.2 1057.6 %reduce-scatter.33.cloned.1.call-start = ((), (), s32[]{:S(2)}) async-start(), calls=%async_computation.49 | async-start | bytes 2654208 | tf_op jit(solution)/shard_map/reduce_scatter | solution.py:530
  879.9 1055.6 %reduce-scatter.17.cloned.1.call-start = ((), (), s32[]{:S(2)}) async-start(), calls=%async_computation.41 | async-start | bytes 2654208 | tf_op jit(solution)/shard_map/reduce_scatter | solution.py:523
  1858.4 89.3 %reduce-scatter.19.cloned.1.call-start = ((), (), s32[]{:S(2)}) async-start(), calls=%async_computation.42 | async-start | bytes 2654208 | tf_op jit(solution)/shard_map/reduce_scatter | solution.py:524
  1884.7 109.1 %reduce-scatter.15.cloned.1.call-start = ((), (), s32[]{:S(2)}) async-start(), calls=%async_computation.40 | async-start | bytes 2654208 | tf_op jit(solution)/shard_map/reduce_scatter | solution.py:522
  1910.7 163.1 %reduce-scatter.23.cloned.1.call-start = ((), (), s32[]{:S(2)}) async-start(), calls=%async_computation.44 | async-start | bytes 10616832 | tf_op jit(solution)/shard_map/reduce_scatter | solution.py:528
  1919.5 234.3 %reduce-scatter.25.cloned.1.call-start = ((), (), s32[]{:S(2)}) async-start(), calls=%async_computation.45 | async-start | bytes 10616832 | tf_op jit(solution)/shard_map/reduce_scatter | solution.py:529
  1930.5 316.2 %all-reduce.20.cloned.1.call-start = ((), (), s32[]{:S(2)}) async-start(), calls=%async_computation.54 | async-start | bytes 4128768 | tf_op jit(solution)/shard_map/psum | solution.py:556
  2076.0 80.0 %copy-start.25 = (bf16[2048,3,64]{0,2,1:T(8,128)(2,1)S(1)}, bf16[2048,3,64]{0,2,1:T(8,128)(2,1)}, u32[]{:S(2)}) copy-start(bf16[2048,3,64]{0,2,1:T(8,128)(2,1)} %copy-done.24) | copy-start | bytes 2359300
  2076.0 80.0 %copy-start.47 = (f32[3,3,2048]{2,1,0:T(4,128)S(1)}, f32[3,3,2048]{2,1,0:T(4,128)}, u32[]{:S(2)}) copy-start(f32[3,3,2048]{2,1,0:T(4,128)} %copy-done.46) | copy-start | bytes 221188
  2076.0 80.0 %copy-start.69 = (f32[3,3,2048]{2,1,0:T(4,128)S(1)}, f32[3,3,2048]{2,1,0:T(4,128)}, u32[]{:S(2)}) copy-start(f32[3,3,2048]{2,1,0:T(4,128)} %copy-done.68) | copy-start | bytes 221188
  2076.0 80.1 %copy-start.84 = (f32[3,3]{1,0:T(4,128)S(1)}, f32[3,3]{1,0:T(4,128)}, u32[]{:S(2)}) copy-start(f32[3,3]{1,0:T(4,128)} %copy-done.83) | copy-start | bytes 112
  2076.0 80.1 %copy-start.92 = (f32[3,3]{1,0:T(4,128)S(1)}, f32[3,3]{1,0:T(4,128)}, u32[]{:S(2)}) copy-start(f32[3,3]{1,0:T(4,128)} %copy-done.91) | copy-start | bytes 112
  2156.0 136.2 %reduce-scatter.31.cloned.1.call-start = ((), (), s32[]{:S(2)}) async-start(), calls=%async_computation.48 | async-start | bytes 2654208 | tf_op jit(solution)/shard_map/reduce_scatter | solution.py:536
  2170.7 168.0 %reduce-scatter.29.cloned.1.call-start = ((), (), s32[]{:S(2)}) async-start(), calls=%async_computation.47 | async-start | bytes 2654208 | tf_op jit(solution)/shard_map/reduce_scatter | solution.py:534
  2174.6 210.7 %reduce-scatter.27.cloned.1.call-start = ((), (), s32[]{:S(2)}) async-start(), calls=%async_computation.46 | async-start | bytes 2654208 | tf_op jit(solution)/shard_map/reduce_scatter | solution.py:533
  2178.4 253.1 %reduce-scatter.37.cloned.1.call-start = ((), (), s32[]{:S(2)}) async-start(), calls=%async_computation.51 | async-start | bytes 2654208 | tf_op jit(solution)/shard_map/reduce_scatter | solution.py:537
  2181.2 331.4 %reduce-scatter.39.cloned.1.call-start = ((), (), s32[]{:S(2)}) async-start(), calls=%async_computation.52 | async-start | bytes 10616832 | tf_op jit(solution)/shard_map/reduce_scatter | solution.py:539
  2187.1 406.5 %reduce-scatter.41.cloned.1.call-start = ((), (), s32[]{:S(2)}) async-start(), calls=%async_computation.53 | async-start | bytes 10616832 | tf_op jit(solution)/shard_map/reduce_scatter | solution.py:540
  (147 other events, 1379.2 us)
Sparse Core Ops, SparseCore 0:
  9.9 26.9 all-gather.16
  38.8 24.0 all-gather.18
  64.8 24.0 all-gather.20
  90.6 24.0 all-gather.22
  116.4 38.9 all-gather.24
  157.1 38.9 all-gather.26
  197.9 24.0 all-gather.36
  223.9 24.0 all-gather.32
  249.9 24.0 all-gather.28
  275.7 24.0 all-gather.30
  301.7 24.0 all-gather.34
  327.5 24.0 all-gather.38
  353.5 38.9 all-gather.40
  394.2 38.9 all-gather.42
  835.1 45.9 reduce-scatter.34
  884.7 42.4 reduce-scatter.20
  930.4 42.4 reduce-scatter.32
  1858.5 43.2 reduce-scatter.16
  1905.2 42.4 reduce-scatter.18
  1951.3 42.4 reduce-scatter.14
  1997.3 76.4 reduce-scatter.22
  2077.3 76.4 reduce-scatter.24
  2157.9 88.6 all-reduce.19
  2250.8 41.3 reduce-scatter.30
  2296.2 42.4 reduce-scatter.28
  2342.8 42.4 reduce-scatter.26
  2389.1 42.4 reduce-scatter.36
  2436.0 76.4 reduce-scatter.38
  2517.1 76.4 reduce-scatter.40
where the time goes:
time: 2610 us; the launch traced here: 2600 us
  local copies, waits for them, and re-layouts  1130 us (43%)
  waiting for transfers between devices  665 us (25%)
  matrix products  338 us (13%)
  other arithmetic  180 us (7%)
  blocking collectives  176 us (7%)
  loops' own time  54.1 us (2%)
  starting transfers between devices  38.4 us (1%)
    while x132, local copies, waits for them, and re-layouts  729 us
    reshape x12, local copies, waits for them, and re-layouts, bias_block(): repeated[:, block_rows:block_rows + block_rows * (length_all - 1)]  230 us
    dot_general x8, matrix products, block_scores(): jnp.einsum('qhe,khe->hqk', rows_query, key_heads, preferred_element_type=...  86.5 us
    reduce_scatter x1, waiting for transfers between devices, body(): lax.psum_scatter(grad_dff_out, 'fsdp', scatter_dimension=0, tiled=True)  81 us
    reduce_scatter x1, waiting for transfers between devices, body(): lax.psum_scatter(grad_dff_in, 'fsdp', scatter_dimension=0, tiled=True)  81 us
    reduce_scatter x1, waiting for transfers between devices, body(): lax.psum_scatter(grad_ff_in, 'fsdp', scatter_dimension=0, tiled=True)  78.4 us
    reduce_scatter x1, waiting for transfers between devices, body(): lax.psum_scatter(grad_ff_out, 'fsdp', scatter_dimension=0, tiled=True)  77.8 us
    slice x8, local copies, waits for them, and re-layouts, bias_block(): repeated[:, block_rows:block_rows + block_rows * (length_all - 1)]  74.9 us
  transfers between devices with their start and end apart: 38, of which 21 were waited for; matrix products, arithmetic and copies ran while one was open for 62% of the time, Pallas kernels for 0%

commit v1 on v0

v1 whole, which is shorter than its diff:
```python
import functools, math
import jax, jax.numpy as jnp
from jax import lax
from jax.experimental import pallas as pl
from jax.experimental.pallas import tpu as pltpu
from jax.sharding import PartitionSpec as P

HEADS=12; HEAD=64; BUCKETS=32
LIMITS = (12, 16, 23, 32, 46, 64, 91)
BLK=256
SUB=128
BAND=512
NEG=-1e30

def bucket_of(relative):
    distance = jnp.abs(relative)
    bucket = jnp.minimum(distance, 8)
    for bound_value in LIMITS:
        bucket = bucket + (distance >= bound_value).astype(jnp.int32)
    return bucket + 16 * (relative > 0).astype(jnp.int32)

def nt(a,b):
    return lax.dot_general(a,b,(((1,),(1,)),((),())),preferred_element_type=jnp.float32)
def tn(a,b):
    return lax.dot_general(a,b,(((0,),(0,)),((),())),preferred_element_type=jnp.float32)
def nn(a,b):
    return lax.dot_general(a,b,(((1,),(0,)),((),())),preferred_element_type=jnp.float32)

def band_offsets(sign):
    c = jnp.arange(BAND, dtype=jnp.int32)
    t = jnp.where(c < 3*SUB, c, c - BAND) - SUB
    return sign * t

def seg_of(pos, e0, e1):
    return (pos >= e0).astype(jnp.int32) + (pos >= e1).astype(jnp.int32)

def build_tiles(band_ref, tiles, hh, flip):
    row = band_ref[hh:hh+1, :]
    x = jnp.broadcast_to(row, (SUB, BAND))
    x = pltpu.roll(x, 0, 1, stride=1, stride_axis=0)
    last, first = row[0:1, 3*SUB-1:3*SUB], row[0:1, 3*SUB:3*SUB+1]
    near = [x[:, n*SUB:(n+1)*SUB] for n in range(3)]
    if flip:
        near = near[::-1]
        last, first = first, last
    low = jnp.broadcast_to(first, (SUB, SUB))
    high = jnp.broadcast_to(last, (SUB, SUB))
    for d in range(5):
        for r in range(2):
            for c in range(2):
                off = ((r - c) if flip else (c - r)) + 2*(d-2)
                tiles[hh, d, r*SUB:(r+1)*SUB, c*SUB:(c+1)*SUB] = low if off < -1 else high if off > 1 else near[off+1]

def fwd_kernel(info, band_ref, q_ref, k_ref, v_ref, ctx_ref, lse_ref, tiles, s_scr):
    p0, e0, e1 = info[0], info[1], info[2]
    T = q_ref.shape[0]; G = k_ref.shape[0]
    lane = lax.broadcasted_iota(jnp.int32, (1,128), 1)
    left = lane < HEAD
    for hh in range(2):
        build_tiles(band_ref, tiles, hh, False)
    for i in range(T//BLK):
        a = p0 + i*BLK; b = a + BLK - 1
        lo = jnp.where(a >= e1, e1, jnp.where(a >= e0, e0, 0))
        hi = jnp.where(b >= e1, G, jnp.where(b >= e0, e1, e0))
        j0 = lo // BLK; j1 = (hi + BLK - 1)//BLK
        ib = a // BLK
        qb = q_ref[i*BLK:(i+1)*BLK, :]
        row_pos = a + lax.broadcasted_iota(jnp.int32, (BLK,1), 0)
        row_seg = jnp.broadcast_to(seg_of(row_pos, e0, e1),(BLK,128))
        zero = jnp.zeros_like(qb)
        qh = [jnp.where(left, qb, zero), jnp.where(left, zero, qb)]
        def score(j, carry):
            koff = pl.multiple_of(j*BLK, BLK)
            kb = k_ref[pl.ds(koff, BLK), :]
            kpos = koff + lax.broadcasted_iota(jnp.int32, (1,BLK), 1)
            kseg = seg_of(kpos, e0, e1)
            same = jnp.concatenate([row_seg == kseg[:, :128], row_seg == kseg[:,128:]],axis=1)
            d = jnp.clip(j - ib, -2, 2) + 2
            out = []
            for hh in range(2):
                s = nt(qh[hh], kb) + tiles[hh, d]
                s = jnp.where(same, s, NEG)
                s_scr[hh, j] = s
                out.append(jnp.maximum(carry[hh], jnp.maximum(s[:, :128], s[:, 128:])))
            return tuple(out)
        init = jnp.full((BLK,128), NEG, jnp.float32)
        mx = lax.fori_loop(j0, j1, score, (init, init))
        top = [jnp.max(m, axis=1, keepdims=True) for m in mx]
        def weigh(j, carry):
            koff = pl.multiple_of(j*BLK, BLK)
            vb = v_ref[pl.ds(koff, BLK), :]
            one = jnp.ones_like(vb)
            vh = [jnp.where(left, vb, one), jnp.where(left, one, vb)]
            out = []
            for hh in range(2):
                p = jnp.exp(s_scr[hh, j] - top[hh]).astype(jnp.bfloat16)
                out.append(carry[hh] + nn(p, vh[hh]))
            return tuple(out)
        zf = jnp.zeros((BLK,128), jnp.float32)
        acc = lax.fori_loop(j0, j1, weigh, (zf, zf))
        tot = [jnp.where(left, pltpu.roll(acc[0], HEAD, 1), pltpu.roll(acc[1], HEAD, 1))]
        num = jnp.where(left, acc[0], acc[1])
        total = tot[0]
        ctx_ref[i*BLK:(i+1)*BLK, :] = (num / total).astype(jnp.bfloat16)
        lse_ref[i*BLK:(i+1)*BLK, :] = jnp.where(left, top[0], top[1]) + jnp.log(total)

def attn_fwd(info, band, q, k, v):
    T=q.shape[0]; G=k.shape[0]; W=q.shape[1]
    pairs=W//128
    return pl.pallas_call(
        fwd_kernel,
        grid=(pairs,),
        in_specs=[pl.BlockSpec(memory_space=pltpu.SMEM),
                  pl.BlockSpec((None,2,BAND), lambda p:(p,0,0)),
                  pl.BlockSpec((T,128), lambda p:(0,p)),
                  pl.BlockSpec((G,128), lambda p:(0,p)),
                  pl.BlockSpec((G,128), lambda p:(0,p))],
        out_specs=[pl.BlockSpec((T,128), lambda p:(0,p)), pl.BlockSpec((T,128), lambda p:(0,p))],
        out_shape=[jax.ShapeDtypeStruct((T,W), jnp.bfloat16), jax.ShapeDtypeStruct((T,W), jnp.float32)],
        scratch_shapes=[pltpu.VMEM((2,5,BLK,BLK), jnp.float32), pltpu.VMEM((2,G//BLK,BLK,BLK), jnp.float32)],
        compiler_params=pltpu.CompilerParams(vmem_limit_bytes=50<<20),
        cost_estimate=pl.CostEstimate(flops=4*HEADS*T*1280*128, bytes_accessed=4*G*W+8*T*W, transcendentals=HEADS*T*1280),
    )(info, band, q, k, v)

def bwd_kernel(info, band_ref, q_ref, k_ref, v_ref, g_ref, ctx_ref, lse_ref, gq_ref, gk_ref, gv_ref, gb_ref, gf_ref, tiles, gt, gk_acc, gv_acc):
    p0, e0, e1 = info[0], info[1], info[2]
    T = q_ref.shape[0]; G = k_ref.shape[0]
    lane = lax.broadcasted_iota(jnp.int32, (1,128), 1)
    left = lane < HEAD
    sub_left = lax.broadcasted_iota(jnp.int32, (128,1), 0) < HEAD
    for hh in range(2):
        build_tiles(band_ref, tiles, hh, True)
    gt[...] = jnp.zeros_like(gt)
    gk_acc[...] = jnp.zeros_like(gk_acc)
    gv_acc[...] = jnp.zeros_like(gv_acc)
    for i in range(T//BLK):
        a = p0 + i*BLK; b = a + BLK - 1
        lo = jnp.where(a >= e1, e1, jnp.where(a >= e0, e0, 0))
        hi = jnp.where(b >= e1, G, jnp.where(b >= e0, e1, e0))
        j0 = lo // BLK; j1 = (hi + BLK - 1)//BLK
        ib = a // BLK
        rows = slice(i*BLK,(i+1)*BLK)
        qb = q_ref[rows, :]; gb = g_ref[rows, :]
        zero = jnp.zeros_like(qb)
        qh = [jnp.where(left, qb, zero), jnp.where(left, zero, qb)]
        gh = [jnp.where(left, gb, zero), jnp.where(left, zero, gb)]
        prod = (gb.astype(jnp.float32) * ctx_ref[rows,:].astype(jnp.float32)).T
        lse_t = lse_ref[rows,:].T
        dot = [jnp.sum(prod[hh*HEAD:(hh+1)*HEAD], axis=0, keepdims=True) for hh in range(2)]
        lse = [lse_t[hh*HEAD:hh*HEAD+1] for hh in range(2)]
        q_pos = a + lax.broadcasted_iota(jnp.int32, (1,BLK), 1)
        q_seg = seg_of(q_pos, e0, e1)
        def step(j, carry):
            koff = pl.multiple_of(j*BLK, BLK)
            kb = k_ref[pl.ds(koff, BLK), :]
            vb = v_ref[pl.ds(koff, BLK), :]
            kpos = koff + lax.broadcasted_iota(jnp.int32, (BLK,1), 0)
            same = jnp.broadcast_to(seg_of(kpos, e0, e1), (BLK,BLK)) == jnp.broadcast_to(q_seg, (BLK,BLK))
            d = jnp.clip(j - ib, -2, 2) + 2
            gqs=[]
            gk = None; gv=None
            for hh in range(2):
                s = nt(kb, qh[hh]) + tiles[hh, d]
                s = jnp.where(same, s, NEG)
                p = jnp.exp(s - lse[hh])
                gp = nt(vb, gh[hh])
                gs = p * (gp - dot[hh])
                gt[hh, d] += gs
                pb = p.astype(jnp.bfloat16); gsb = gs.astype(jnp.bfloat16)
                tk = nn(gsb, qh[hh]); tv = nn(pb, gh[hh])
                gk = tk if gk is None else gk + tk
                gv = tv if gv is None else gv + tv
                gqs.append(carry[hh] + tn(gsb, kb))
            gk_acc[pl.ds(koff,BLK), :] += gk
            gv_acc[pl.ds(koff,BLK), :] += gv
            return tuple(gqs)
        zf = jnp.zeros((BLK,128), jnp.float32)
        gq = lax.fori_loop(j0, j1, step, (zf, zf))
        gq_ref[rows,:] = jnp.where(left, gq[0], gq[1]).astype(jnp.bfloat16)
    gk_ref[...] = gk_acc[...].astype(jnp.bfloat16)
    gv_ref[...] = gv_acc[...].astype(jnp.bfloat16)
    for hh in range(2):
        near = [None]*3; low = None; high = None
        for d in range(5):
            for r in range(2):
                for c in range(2):
                    off = r - c + 2*(d-2)
                    x = gt[hh, d, r*SUB:(r+1)*SUB, c*SUB:(c+1)*SUB]
                    if off < -1: low = x if low is None else low + x
                    elif off > 1: high = x if high is None else high + x
                    else: near[off+1] = x if near[off+1] is None else near[off+1] + x
        x = jnp.concatenate([near[2], near[1], near[0], jnp.zeros((SUB,SUB),jnp.float32)], axis=1)
        rows_left = SUB
        while rows_left > 1:
            rows_left //= 2
            x = x[:rows_left] + pltpu.roll(x[rows_left:], BAND - rows_left, 1)
        gb_ref[hh:hh+1,:] = x
        gf_ref[hh:hh+1,:] = jnp.concatenate([jnp.sum(low, axis=0, keepdims=True), jnp.sum(high, axis=0, keepdims=True)], axis=1)

def attn_bwd(info, band, q, k, v, g, ctx, lse):
    T=q.shape[0]; G=k.shape[0]; W=q.shape[1]
    pairs=W//128
    tb = lambda: pl.BlockSpec((T,128), lambda p:(0,p))
    gb = lambda: pl.BlockSpec((G,128), lambda p:(0,p))
    return pl.pallas_call(
        bwd_kernel,
        grid=(pairs,),
        in_specs=[pl.BlockSpec(memory_space=pltpu.SMEM),
                  pl.BlockSpec((None,2,BAND), lambda p:(p,0,0)),
                  tb(), gb(), gb(), tb(), tb(), tb()],
        out_specs=[tb(), gb(), gb(), pl.BlockSpec((None,2,BAND), lambda p:(p,0,0)), pl.BlockSpec((None,2,2*SUB), lambda p:(p,0,0))],
        out_shape=[jax.ShapeDtypeStruct((T,W), jnp.bfloat16), jax.ShapeDtypeStruct((G,W), jnp.bfloat16), jax.ShapeDtypeStruct((G,W), jnp.bfloat16),
                   jax.ShapeDtypeStruct((pairs,2,BAND), jnp.float32), jax.ShapeDtypeStruct((pairs,2,2*SUB), jnp.float32)],
        scratch_shapes=[pltpu.VMEM((2,5,BLK,BLK), jnp.float32), pltpu.VMEM((2,5,BLK,BLK), jnp.float32),
                        pltpu.VMEM((G,128), jnp.float32), pltpu.VMEM((G,128), jnp.float32)],
        compiler_params=pltpu.CompilerParams(vmem_limit_bytes=50<<20),
        cost_estimate=pl.CostEstimate(flops=10*HEADS*T*1280*128, bytes_accessed=8*G*W+12*T*W, transcendentals=HEADS*T*1280),
    )(info, band, q, k, v, g, ctx, lse)

def make_band(table, sign):
    off = band_offsets(sign)
    oh = (bucket_of(off)[None,:] == jnp.arange(BUCKETS, dtype=jnp.int32)[:,None]).astype(jnp.bfloat16)
    return jnp.dot(table, oh, preferred_element_type=jnp.float32).reshape(HEADS//2, 2, BAND)

def table_grad(gb, gf):
    oh = (bucket_of(band_offsets(-1))[:,None] == jnp.arange(BUCKETS, dtype=jnp.int32)[None,:]).astype(jnp.float32)
    t = jnp.dot(gb.reshape(HEADS,BAND), oh, precision=lax.Precision.HIGHEST)
    f = gf.reshape(HEADS, 2, SUB).sum(axis=2)
    return t.at[:,15].add(f[:,0]).at[:,31].add(f[:,1])


eps = 1e-06
GELU_COEF = 0.044715
GELU_ROOT = math.sqrt(2.0 / math.pi)
bf16 = jnp.bfloat16
f32 = jnp.float32


def gelu_both(values):
    inner = GELU_ROOT * (values + GELU_COEF * values * values * values)
    tanh_val = jnp.tanh(inner)
    half = 0.5 * (1.0 + tanh_val)
    slope = half + 0.5 * values * (1.0 - tanh_val * tanh_val) * GELU_ROOT * (
        1.0 + 3.0 * GELU_COEF * values * values
    )
    return values * half, slope


def norm_forward(values, gain_vec):
    inverse = lax.rsqrt(jnp.mean(values * values, axis=-1, keepdims=True) + eps)
    return (values * inverse * gain_vec).astype(bf16), inverse


def norm_backward(values, inverse, gain_vec, grad_normed):
    scaled = grad_normed * gain_vec
    cubed = inverse * inverse * inverse
    grad_values = inverse * scaled - values * cubed * jnp.mean(
        scaled * values, axis=-1, keepdims=True
    )
    return grad_values, jnp.sum(grad_normed * values * inverse, axis=0)


def body(
    tokens, doc_lengths, gain_attn, query_weight, key_weight, value_weight, out_weight, bias_table,
    gain_ff, ff_in, ff_out, gain_self, self_value, self_out, gain_cross, cross_query, cross_key,
    cross_value, cross_out, gain_dff, dff_in, dff_out, enc_cot, dec_cot,
):
    seq_index = lax.axis_index("seq")
    seq_count = lax.axis_size("seq")
    own = lax.axis_index("fsdp")
    fsdp = lax.axis_size("fsdp")
    rows = tokens.shape[0]
    width = tokens.shape[1]
    group_tok = rows * seq_count
    part = query_weight.shape[0]
    buckets_part = bias_table.shape[0]
    docs = doc_lengths.shape[1]

    columns = [gain_attn, gain_ff, gain_self, gain_cross, gain_dff,
               jnp.pad(bias_table, (0, part - buckets_part))]
    small = jnp.pad(jnp.stack(columns, axis=1), ((0, 0), (0, 128 - len(columns))))
    over_fsdp = lambda piece: lax.all_gather(piece, "fsdp", axis=0, tiled=True)
    group = lax.all_gather(tokens, "seq", axis=0, tiled=True)
    first_weights = over_fsdp(jnp.concatenate([query_weight, key_weight, value_weight, small], axis=1))
    second_weights = over_fsdp(jnp.concatenate([out_weight, ff_in], axis=1))
    ff_out_full = over_fsdp(ff_out)
    dec_weights = over_fsdp(jnp.concatenate(
        [self_value, self_out, cross_query, cross_key, cross_value, cross_out, dff_in], axis=1))
    dff_out_full = over_fsdp(dff_out)

    query_full = first_weights[:, :width]
    kv_full = first_weights[:, width : 3 * width]
    vectors = first_weights[:, 3 * width : 3 * width + len(columns)].astype(f32)
    gain_attn_f, gain_ff_f, gain_self_f, gain_cross_f, gain_dff_f = (vectors[:, n] for n in range(5))
    table = vectors[:, 5].reshape(fsdp, part)[:, :buckets_part].reshape(HEADS, BUCKETS).astype(bf16)
    out_full = second_weights[:, :width]
    ff_in_full = second_weights[:, width:]
    self_value_full, self_out_full, cross_query_full, cross_key_full, cross_value_full, cross_out_full = (
        dec_weights[:, n * width : (n + 1) * width] for n in range(6))
    dff_in_full = dec_weights[:, 6 * width :]

    lengths = doc_lengths[0]
    end_zero = lengths[0]
    end_one = lengths[0] + lengths[1]
    here = seq_index * rows
    info = jnp.stack([here.astype(jnp.int32), end_zero, end_one])
    local_seg = seg_of(here + jnp.arange(rows, dtype=jnp.int32), end_zero, end_one)
    starts = jnp.stack([jnp.zeros_like(end_zero), end_zero, end_one])

    group_f = group.astype(f32)
    normed_all, inverse_all = norm_forward(group_f, gain_attn_f)
    normed = lax.dynamic_slice_in_dim(normed_all, here, rows, 0)
    inverse_attn = lax.dynamic_slice_in_dim(inverse_all, here, rows, 0)
    query = nn(normed, query_full).astype(bf16)
    key = nn(normed_all, kv_full[:, :width]).astype(bf16)
    value = nn(normed_all, kv_full[:, width:]).astype(bf16)
    context, lse = attn_fwd(info, make_band(table, 1), query, key, value)
    tokens_f = tokens.astype(f32)
    middle = tokens_f + nn(context, out_full)
    normed_ff, inverse_ff = norm_forward(middle, gain_ff_f)
    pre_act = nn(normed_ff, ff_in_full)
    hidden_f, slope = gelu_both(pre_act)
    hidden = hidden_f.astype(bf16)
    enc_hidden = middle + nn(hidden, ff_out_full)
    memory = enc_hidden.astype(bf16)

    pick = (starts[:, None] == jnp.arange(group_tok, dtype=jnp.int32)[None, :]).astype(bf16)
    first = nn(pick, group)
    self_low, self_inv = norm_forward(first, gain_self_f)
    self_vals = nn(self_low, self_value_full).astype(bf16)
    state_one = first + nn(self_vals, self_out_full)
    cross_low, cross_inv = norm_forward(state_one, gain_cross_f)
    cross_q = nn(cross_low, cross_query_full).astype(bf16)
    head_of = jnp.arange(width, dtype=jnp.int32) // HEAD
    head_mask = (jnp.arange(HEADS, dtype=jnp.int32)[:, None] == head_of[None, :])[:, None, :]

    def by_head(values):
        return jnp.where(head_mask, values[None], 0).reshape(HEADS * docs, width)

    def from_heads(values):
        return jnp.sum(jnp.where(head_mask, values.reshape(HEADS, docs, width), 0), axis=0)

    probe = nt(by_head(cross_q), cross_key_full).astype(bf16)
    doc_rows = jnp.tile(jnp.arange(docs, dtype=jnp.int32), HEADS)
    in_doc = doc_rows[:, None] == local_seg[None, :]
    scores = jnp.where(in_doc, nt(probe, memory), NEG)
    top = jnp.max(scores, axis=1, keepdims=True)
    powers = jnp.where(in_doc, jnp.exp(scores - top), 0.0)
    total = jnp.sum(powers, axis=1, keepdims=True)
    mixed = nn(powers.astype(bf16), memory)
    lanes = lambda column: jnp.broadcast_to(column, (HEADS * docs, 128))
    parts = lax.all_gather(jnp.concatenate([mixed, lanes(top), lanes(total)], axis=1), "seq", axis=0)
    tops = parts[:, :, width : width + 1]
    top_all = jnp.max(tops, axis=0)
    scale = jnp.exp(tops - top_all[None])
    total_all = jnp.sum(scale * parts[:, :, width + 128 : width + 129], axis=0)
    mixed_all = (jnp.sum(scale * parts[:, :, :width], axis=0) / total_all).astype(bf16)
    cross_ctx = from_heads(nn(mixed_all, cross_value_full)).astype(bf16)
    state_two = state_one + nn(cross_ctx, cross_out_full)
    ffn_low, ffn_inv = norm_forward(state_two, gain_dff_f)
    dec_hid_f, dec_slope = gelu_both(nn(ffn_low, dff_in_full))
    dec_hid = dec_hid_f.astype(bf16)
    dec_hidden = state_two + nn(dec_hid, dff_out_full)

    grad_dec_pre = (dec_slope * nt(dec_cot, dff_out_full)).astype(bf16)
    back_values, grad_gain_dff = norm_backward(state_two, ffn_inv, gain_dff_f, nt(grad_dec_pre, dff_in_full))
    grad_two = dec_cot.astype(f32) + back_values
    grad_two_low = grad_two.astype(bf16)
    grad_cross_ctx = nt(grad_two_low, cross_out_full).astype(bf16)
    pull = nt(by_head(grad_cross_ctx), cross_value_full).astype(bf16)
    probs = powers * (jnp.exp(top - top_all) / total_all)
    row_dot = jnp.sum(by_head(grad_cross_ctx.astype(f32) * cross_ctx.astype(f32)), axis=1, keepdims=True)
    grad_scores = (probs * (nt(pull, memory) - row_dot)).astype(bf16)
    grad_memory = tn(jnp.concatenate([grad_scores, probs.astype(bf16)], axis=0),
                     jnp.concatenate([probe, pull], axis=0))
    grad_mixed = lax.psum(nn(grad_scores, memory), "seq").astype(bf16)
    grad_cross_q = from_heads(nn(grad_mixed, cross_key_full)).astype(bf16)
    back_values, grad_gain_cross = norm_backward(state_one, cross_inv, gain_cross_f, nt(grad_cross_q, cross_query_full))
    grad_one = grad_two + back_values
    grad_one_low = grad_one.astype(bf16)
    grad_self_vals = nt(grad_one_low, self_out_full).astype(bf16)
    back_values, grad_gain_self = norm_backward(first, self_inv, gain_self_f, nt(grad_self_vals, self_value_full))
    grad_first = grad_one + back_values

    gains_rows = jnp.stack([grad_gain_self, grad_gain_cross, grad_gain_dff]).astype(bf16)
    pack = [self_low, grad_self_vals, self_vals, grad_one_low, cross_low, grad_cross_q, cross_q, grad_cross_ctx,
            cross_ctx, grad_two_low, ffn_low, dec_cot, gains_rows]
    wide = dec_hid.shape[1] // width
    pack += [dec_hid[:, n * width : (n + 1) * width] for n in range(wide)]
    pack += [grad_dec_pre[:, n * width : (n + 1) * width] for n in range(wide)]
    pack += [grad_mixed, mixed_all]
    pack = jnp.concatenate(pack, axis=0)
    pack = jnp.pad(pack, ((0, -pack.shape[0] % 16), (0, 0)))
    packs = lax.all_gather(pack, "fsdp", axis=0)
    rowset = lambda n: packs[:, n * docs : (n + 1) * docs].reshape(fsdp * docs, width)
    mine = lambda values: lax.dynamic_slice_in_dim(values, own * part, part, 1)
    shard_self_value = tn(mine(rowset(0)), rowset(1))
    shard_self_out = tn(mine(rowset(2)), rowset(3))
    shard_cross_query = tn(mine(rowset(4)), rowset(5))
    shard_cross_out = tn(mine(rowset(8)), rowset(9))
    at = 13
    hid_all = jnp.concatenate([rowset(at + n) for n in range(wide)], axis=1)
    pre_all = jnp.concatenate([rowset(at + wide + n) for n in range(wide)], axis=1)
    shard_dff_in = tn(mine(rowset(10)), pre_all)
    part_ff = dff_out.shape[0]
    shard_dff_out = tn(lax.dynamic_slice_in_dim(hid_all, own * part_ff, part_ff, 1), rowset(11))
    gains_all = jnp.sum(packs[:, 12 * docs : 13 * docs].astype(f32), axis=0)
    gains_own = mine(gains_all)
    at = (13 + 2 * wide) * docs
    heads_rows = HEADS * docs
    mixed_g = packs[:, at : at + heads_rows].reshape(fsdp * heads_rows, width)
    mixed_m = packs[:, at + heads_rows : at + 2 * heads_rows].reshape(fsdp * heads_rows, width)
    spread = lambda n: jnp.where(head_mask[None], packs[:, None, n * docs : (n + 1) * docs], 0).reshape(
        fsdp * heads_rows, width)
    shard_cross_key = tn(mine(mixed_g), spread(6))
    shard_cross_value = tn(mine(mixed_m), spread(7))

    grad_enc = enc_cot.astype(f32) + grad_memory
    grad_enc_low = grad_enc.astype(bf16)
    scatter = lambda values: lax.psum(
        lax.psum_scatter(values.astype(bf16), "fsdp", scatter_dimension=0, tiled=True), "seq").astype(f32)
    shard_ff_out = scatter(tn(hidden, grad_enc_low))
    grad_pre = (slope * nt(grad_enc_low, ff_out_full)).astype(bf16)
    shard_ff_in = scatter(tn(normed_ff, grad_pre))
    back_values, grad_gain_ff = norm_backward(middle, inverse_ff, gain_ff_f, nt(grad_pre, ff_in_full))
    grad_middle = grad_enc + back_values
    grad_middle_low = grad_middle.astype(bf16)
    grad_out = tn(context, grad_middle_low)
    grad_context = nt(grad_middle_low, out_full).astype(bf16)
    grad_query, grad_key, grad_value, grad_band, grad_far = attn_bwd(
        info, make_band(table, -1), query, key, value, grad_context, context, lse)
    grad_table = table_grad(grad_band, grad_far).reshape(fsdp, buckets_part)
    partial = nt(grad_key, kv_full[:, :width]) + nt(grad_value, kv_full[:, width:])
    grad_normed = nt(grad_query, query_full) + lax.psum_scatter(
        partial.astype(bf16), "seq", scatter_dimension=0, tiled=True).astype(f32)
    back_values, grad_gain_attn = norm_backward(tokens_f, inverse_attn, gain_attn_f, grad_normed)
    local_pick = lax.dynamic_slice_in_dim(pick, here, rows, 1).astype(f32)
    first_back = lax.dot_general(local_pick, grad_first, (((0,), (0,)), ((), ())),
                                 precision=lax.Precision.HIGHEST, preferred_element_type=f32)
    tokens_grad = grad_middle + back_values + first_back
    small_grads = [grad_gain_attn, grad_gain_ff,
                   jnp.pad(grad_table, ((0, 0), (0, part - buckets_part))).reshape(width)]
    small_grads = jnp.pad(jnp.stack(small_grads, axis=1), ((0, 0), (0, 125)))
    last = scatter(jnp.concatenate([
        tn(normed, grad_query).astype(bf16), tn(normed_all, grad_key).astype(bf16),
        tn(normed_all, grad_value).astype(bf16), grad_out.astype(bf16), small_grads.astype(bf16)], axis=1))
    shard_query, shard_key, shard_value, shard_out = (last[:, n * width : (n + 1) * width] for n in range(4))
    tail = last[:, 4 * width :]
    return (
        enc_hidden, dec_hidden, tokens_grad, tail[:, 0], shard_query, shard_key, shard_value, shard_out,
        tail[:buckets_part, 2], tail[:, 1], shard_ff_in, shard_ff_out, gains_own[0], shard_self_value, shard_self_out,
        gains_own[1], shard_cross_query, shard_cross_key, shard_cross_value, shard_cross_out, gains_own[2],
        shard_dff_in, shard_dff_out,
    )


def solution(mesh):
    tok, wide, one = P(("fsdp", "seq"), None), P("fsdp", None), P("fsdp")
    return jax.shard_map(
        body,
        mesh=mesh,
        in_specs=(tok, wide, one, wide, wide, wide, wide, one, one, wide, wide, one, wide, wide, one, wide, wide, wide,
                  wide, one, wide, wide, tok, wide),
        out_specs=(tok, wide, tok, one, wide, wide, wide, wide, one, one, wide, wide, one, wide, wide, one, wide, wide,
                   wide, wide, one, wide, wide),
        check_vma=False,
    )
```

time: 2610 us -> 791 us (0.30)
  local copies, waits for them, and re-layouts: 1130 us -> 52.6 us
  waiting for transfers between devices: 665 us -> 425 us
  matrix products: 338 us -> 140 us
  other arithmetic: 180 us -> 26.7 us
  blocking collectives: 176 us -> 39.9 us
  Pallas kernels: 0 us -> 83.1 us
  loops' own time: 54.1 us -> 0 us
  starting transfers between devices: 38.4 us -> 0.49 us
    while x132 -> x0, local copies, waits for them, and re-layouts: 729 us -> none
    reduce_scatter x14 -> x3, waiting for transfers between devices: 550 us -> 142 us  [the longest x2 113 us: body(): lax.psum_scatter(values.astype(bf16), 'fsdp', scatter_dimension=0, tiled=...]
    reshape x24 -> x25, local copies, waits for them, and re-layouts: 239 us -> 15.7 us  [the longest x18 13.8 us: body(): packs[:, n * docs:(n + 1) * docs].reshape(fsdp * docs, width)]
    dot_general x90 -> x52, matrix products: 338 us -> 140 us  [the longest x16 46.5 us: nt(): lax.dot_general(a, b, (((1,), (1,)), ((), ())), preferred_element_type=jn...]
    all_gather x14 -> x7, waiting for transfers between devices: 22.4 us -> 183 us  [the longest x5 127 us: body(): over_fsdp = lambda piece: lax.all_gather(piece, 'fsdp', axis=0, tiled=True)]
    all_to_all x9 -> x0, waiting for transfers between devices: 83.4 us -> none  [the longest x1 19.6 us: body(): lax.all_to_all(context_heads, 'seq', split_axis=0, concat_axis=1, tiled=T...]
    pallas_call x0 -> x2, Pallas kernels: none -> 83.1 us  [the longest x1 51.4 us: attn_bwd(): pl.pallas_call(bwd_kernel, grid=(pairs,), in_specs=[pl.BlockSpec(memory_s...]
    psum x1, waiting for transfers between devices: 0.27 us -> 74.6 us  [body(): lax.psum(lax.psum_scatter(values.astype(bf16), 'fsdp', scatter_dimension=...]
  transfers between devices with their start and end apart: 38 -> 12, of which waited for: 21 -> 10; matrix products, arithmetic and copies ran while one was open for 62% -> 21% of each run, Pallas kernels for 0% -> 4%
where the time goes in v1:
time: 791 us; the launch traced here: 785 us
  waiting for transfers between devices  425 us (54%)
  matrix products  140 us (18%)
  Pallas kernels  83.1 us (11%)
  local copies, waits for them, and re-layouts  52.6 us (7%)
  blocking collectives  39.9 us (5%)
  other arithmetic  26.7 us (3%)
  between operations  17.1 us (2%)
    all_gather x5, waiting for transfers between devices, body(): over_fsdp = lambda piece: lax.all_gather(piece, 'fsdp', axis=0, tiled=True)  127 us
    reduce_scatter x2, waiting for transfers between devices, body(): lax.psum_scatter(values.astype(bf16), 'fsdp', scatter_dimension=0, tiled=...  113 us
    psum x1, waiting for transfers between devices, body(): lax.psum(lax.psum_scatter(values.astype(bf16), 'fsdp', scatter_dimension=...  74.6 us
    all_gather x1, waiting for transfers between devices, body(): group = lax.all_gather(tokens, 'seq', axis=0, tiled=True)  55.5 us
    pallas_call x1, Pallas kernels, attn_bwd(): pl.pallas_call(bwd_kernel, grid=(pairs,), in_specs=[pl.BlockSpec(memory_s...  51.4 us
    dot_general x16, matrix products, nt(): lax.dot_general(a, b, (((1,), (1,)), ((), ())), preferred_element_type=jn...  46.5 us
    dot_general x17, matrix products, nn(): lax.dot_general(a, b, (((1,), (0,)), ((), ())), preferred_element_type=jn...  45 us
    dot_general x15, matrix products, tn(): lax.dot_general(a, b, (((0,), (0,)), ((), ())), preferred_element_type=jn...  44.7 us
  transfers between devices with their start and end apart: 12, of which 10 were waited for; matrix products, arithmetic and copies ran while one was open for 21% of the time, Pallas kernels for 4%

profile of v1, /device:TPU:0, one launch (start us, length us, event | category | flops | bytes accessed | tf_op | source)
XLA Modules:
  0.0 785.0 jit_solution(15027703229512484450)
XLA Ops:
  9.6 1.9 fusion.61
  11.6 2.0 pad_maximum_fusion
  20.4 55.5 %all-gather.13.cloned.1.call-done = bf16[2048,768]{1,0:T(8,128)(2,1)} async-done(((bf16[512,768]{1,0:T(8,128)(2,1)}), bf16[2048,768]{1,0:T(8,128)(2,1)}) %all-gather.13.cloned.1.call-update) | async-done | bytes 3145744 | tf_op jit(solution)/shard_map/all_gather | solution.py:283
  75.9 2.7 fusion
  79.9 31.9 %all-gather.11.cloned.1.call-done = bf16[768,2432]{1,0:T(8,128)(2,1)} async-done(((bf16[96,2432]{1,0:T(8,128)(2,1)}), bf16[768,2432]{1,0:T(8,128)(2,1)}) %all-gather.11.cloned.1.call-update) | async-done | bytes 3735568 | tf_op jit(solution)/shard_map/all_gather | solution.py:282
  115.4 2.8 fusion.2
  118.4 4.1 convolution_convert_fusion.3.k_ref
  123.5 3.9 convolution_convert_fusion.2.v_ref
  127.4 31.7 %shard_map.407 = (bf16[512,768]{1,0:T(8,128)(2,1)S(1)}, f32[512,768]{1,0:T(8,128)S(1)}) custom-call(s32[3]{0:T(128)S(1)} %add_add_fusion.info, f32[6,2,512]{2,1,0:T(2,128)S(1)} %copy.65.band_ref, bf16[512,768]{1,0:T(8,128)(2,1)S(1)} %convolution_convert_fusion.9.q_ref, bf16[2048,768]{1,0:T(8,128)(2,1)} %convolution_convert_fusion.3.k_ref, ...), custom_call_target="tpu_custom_call" | custom-call | flops 4026531840 | bytes 9437184 | tf_op jit(solution)/shard_map/pallas_call | solution.py:110
  160.3 2.2 multiply_reduce_fusion.2
  163.6 6.9 fusion.16
  170.5 28.4 %all-gather.17.cloned.1.call-done = bf16[3072,768]{1,0:T(8,128)(2,1)} async-done(((bf16[384,768]{1,0:T(8,128)(2,1)}), bf16[3072,768]{1,0:T(8,128)(2,1)}) %all-gather.17.cloned.1.call-update) | async-done | bytes 4718608 | tf_op jit(solution)/shard_map/all_gather | solution.py:282
  198.9 9.5 %fusion.171 = (bf16[512,768]{1,0:T(8,128)(2,1)S(1)}, f32[512,768]{1,0:T(8,128)}) fusion(f32[512,768]{1,0:T(8,128)} %copy-done.16, bf16[3072,768]{1,0:T(8,128)(2,1)} %all-gather.17.cloned.1.call-done, f32[512,3072]{1,0:T(8,128)} %fusion.16), kind=kOutput, calls=%fused_computation.310 | convolution fusion | flops 2430861312 | bytes 14942208 | tf_op jit(solution)/shard_map/dot_general | solution.py:27
  208.4 61.1 %all-gather.19.cloned.1.call-done = bf16[768,7680]{1,0:T(8,128)(2,1)} async-done(((bf16[96,7680]{1,0:T(8,128)(2,1)}), bf16[768,7680]{1,0:T(8,128)(2,1)}) %all-gather.19.cloned.1.call-update) | async-done | bytes 11796496 | tf_op jit(solution)/shard_map/all_gather | solution.py:282
  277.9 18.5 %all-gather.2 = f32[4,36,1024]{2,1,0:T(8,128)S(1)} all-gather(f32[1,36,1024]{2,1,0:T(8,128)S(1)} %maximum_bitcast_fusion), channel_id=2, replica_groups=mesh['fsdp'=8,'seq'=4] {'seq'}, dimensions={0}, use_global_device_ids=true | all-gather | bytes 737280 | tf_op jit(solution)/shard_map/all_gather | solution.py:352
  301.0 3.1 multiply_convert_fusion.3
  304.1 6.1 all-gather.21.cloned.1.call-done
  310.2 3.7 fusion.18
  313.9 4.3 multiply_reduce_fusion.3
  326.6 8.8 %fusion.9 = bf16[512,3072]{1,0:T(8,128)(2,1)S(1)} fusion(f32[512,3072]{1,0:T(8,128)} %fusion.16, bf16[3072,768]{1,0:T(8,128)(2,1)} %all-gather.17.cloned.1.call-done, f32[512,768]{1,0:T(8,128)S(1)} %convert_add_fusion.2), kind=kOutput, calls=%fused_computation.13 | convolution fusion | flops 2446196736 | bytes 15728640 | tf_op jit(solution)/shard_map/dot_general | solution.py:23
  335.6 2.9 multiply_reduce_fusion
  339.7 51.4 %shard_map.408 = (bf16[512,768]{1,0:T(8,128)(2,1)S(1)}, bf16[2048,768]{1,0:T(8,128)(2,1)}, bf16[2048,768]{1,0:T(8,128)(2,1)}, f32[6,2,512]{2,1,0:T(2,128)S(1)}, f32[6,2,256]{2,1,0:T(2,128)S(1)}) custom-call(s32[3]{0:T(128)S(1)} %add_add_fusion.info, f32[6,2,512]{2,1,0:T(2,128)S(1)} %copy.67.band_ref, bf16[512,768]{1,0:T(8,128)(2,1)S(1)} %convolution_convert_fusion.9.q_ref, ...), custom_call_target="tpu_custom_call" | custom-call | flops 10066329600 | bytes 17301504 | tf_op jit(solution)/shard_map/pallas_call | solution.py:205
  391.2 4.7 fusion.52
  395.9 4.1 add_convert_fusion
  401.9 21.4 %psum.28 = bf16[36,768]{1,0:T(8,128)(2,1)S(1)} all-reduce(f32[36,768]{1,0:T(8,128)S(1)} %fusion.173), channel_id=1, replica_groups=mesh['fsdp'=8,'seq'=4] {'seq'}, use_global_device_ids=true, to_apply=%region_16.17 | all-reduce | flops 27648 | bytes 165888 | tf_op jit(solution)/shard_map/psum | solution.py:376
  425.1 1.9 multiply_reduce_fusion.4
  429.3 2.5 multiply_reduce_fusion.5
  435.5 3.2 fusion.29
  438.7 5.7 fusion.28
  444.4 3.7 fusion.27
  448.1 1.8 fusion.26
  450.0 29.0 %reduce-scatter.7.cloned.1.call-done = bf16[512,768]{1,0:T(8,128)(2,1)} async-done(((bf16[2048,768]{1,0:T(8,128)(2,1)}), bf16[512,768]{1,0:T(8,128)(2,1)}) %reduce-scatter.7.cloned.1.call-update) | async-done | bytes 786448 | tf_op jit(solution)/shard_map/reduce_scatter | solution.py:434
  479.0 4.5 fusion.25
  484.2 7.5 copy.72
  493.0 6.6 convolution_convert_fusion.1
  501.0 8.3 %convolution_convert_fusion = bf16[3072,768]{1,0:T(8,128)(2,1)} fusion(f32[512,768]{1,0:T(8,128)S(1)} %copy-done.7, f32[512,3072]{1,0:T(8,128)} %fusion.16), kind=kOutput, calls=%fused_computation.17 | convolution fusion | flops 2432827392 | bytes 12582912 | tf_op jit(solution)/shard_map/dot_general | solution.py:25
  511.7 3.7 convolution_add_fusion.1
  516.4 3.0 fusion.165
  543.5 24.3 %reduce-scatter.13.cloned.1.call-done = bf16[96,3200]{1,0:T(8,128)(2,1)} async-done(((bf16[768,3200]{1,0:T(8,128)(2,1)}), bf16[96,3200]{1,0:T(8,128)(2,1)}) %reduce-scatter.13.cloned.1.call-update) | async-done | bytes 614416
  567.8 2.3 copy.73
  570.1 55.3 %reduce-scatter.9.cloned.1.call-done = bf16[96,3072]{1,0:T(8,128)(2,1)} async-done(((bf16[768,3072]{1,0:T(8,128)(2,1)}), bf16[96,3072]{1,0:T(8,128)(2,1)}) %reduce-scatter.9.cloned.1.call-update) | async-done | bytes 589840 | tf_op jit(solution)/shard_map/reduce_scatter | solution.py:421
  625.4 57.4 %reduce-scatter.11.cloned.1.call-done = bf16[384,768]{1,0:T(8,128)(2,1)} async-done(((bf16[3072,768]{1,0:T(8,128)(2,1)}), bf16[384,768]{1,0:T(8,128)(2,1)}) %reduce-scatter.11.cloned.1.call-update) | async-done | bytes 589840 | tf_op jit(solution)/shard_map/reduce_scatter | solution.py:421
  682.8 1.9 fusion.126
  684.7 1.8 fusion.124
  686.5 2.0 fusion.91
  688.5 2.0 fusion.89
  691.9 3.2 fusion.22
  695.1 74.6 %all-reduce.8.cloned.1.call-done = (bf16[96,3200]{0,1:T(8,128)(2,1)}, bf16[96,3072]{1,0:T(8,128)(2,1)}, bf16[384,768]{1,0:T(8,128)(2,1)}) async-done(((bf16[96,3200]{0,1:T(8,128)(2,1)}, bf16[96,3072]{1,0:T(8,128)(2,1)}, bf16[384,768]{1,0:T(8,128)(2,1)}), (bf16[96,3200]{0,1:T(8,128)(2,1)}, bf16[96,3072]{1,0:T(8,128)(2,1)}, bf16[384,768]{1,0:T(8,128)(2,1)})) %all-reduce.8.cloned.1.call-update) | async-done | bytes 1794064 | tf_op jit(solution)/shard_map/psum | solution.py:420
  (367 shorter events, 88.6 us)
Async XLA Ops:
  7.3 68.6 %all-gather.13.cloned.1.call-start = ((), (), s32[]{:S(2)}) async-start(), calls=%async_computation.5 | async-start | bytes 3932160 | tf_op jit(solution)/shard_map/all_gather | solution.py:283
  8.0 103.8 %all-gather.11.cloned.1.call-start = ((), (), s32[]{:S(2)}) async-start(), calls=%async_computation.4 | async-start | bytes 4202496 | tf_op jit(solution)/shard_map/all_gather | solution.py:282
  11.5 148.8 %all-gather.15.cloned.1.call-start = ((), (), s32[]{:S(2)}) async-start(), calls=%async_computation.6 | async-start | bytes 6635520 | tf_op jit(solution)/shard_map/all_gather | solution.py:282
  13.6 185.3 %all-gather.17.cloned.1.call-start = ((), (), s32[]{:S(2)}) async-start(), calls=%async_computation.7 | async-start | bytes 5308416 | tf_op jit(solution)/shard_map/all_gather | solution.py:282
  14.2 255.3 %all-gather.19.cloned.1.call-start = ((), (), s32[]{:S(2)}) async-start(), calls=%async_computation.8 | async-start | bytes 13271040 | tf_op jit(solution)/shard_map/all_gather | solution.py:282
  15.6 294.6 %all-gather.21.cloned.1.call-start = ((), (), s32[]{:S(2)}) async-start(), calls=%async_computation.9 | async-start | bytes 5308416 | tf_op jit(solution)/shard_map/all_gather | solution.py:282
  16.2 462.8 %reduce-scatter.7.cloned.1.call-start = ((), (), s32[]{:S(2)}) async-start(), calls=%async_computation.10 | async-start | bytes 3932160 | tf_op jit(solution)/shard_map/reduce_scatter | solution.py:434
  16.3 99.0 %copy-start.76 = (s32[512]{0:T(512)}, s32[512]{0:T(512)S(1)}, u32[]{:S(2)}) copy-start(s32[512]{0:T(512)S(1)} %get-tuple-element.225) | copy-start | bytes 6148
  20.3 59.1 %copy-start.83 = (s32[3]{0:T(128)}, s32[3]{0:T(128)S(1)}, u32[]{:S(2)}) copy-start(s32[3]{0:T(128)S(1)} %add_add_fusion.1) | copy-start | bytes 40
  20.4 257.0 %copy-start.65 = (s32[36]{0:T(128)}, s32[36]{0:T(128)S(1)}, u32[]{:S(2)}) copy-start(s32[36]{0:T(128)S(1)} %eq.133) | copy-start | bytes 436
  78.7 39.5 %copy-start.55 = (f32[2048]{0:T(1024)}, f32[2048]{0:T(1024)S(1)}, u32[]{:S(2)}) copy-start(f32[2048]{0:T(1024)S(1)} %add_rsqrt_fusion) | copy-start | bytes 24580
  79.9 43.4 %copy-start.78 = (f32[3]{0:T(128)}, f32[3]{0:T(128)S(1)}, u32[]{:S(2)}) copy-start(f32[3]{0:T(128)S(1)} %get-tuple-element.197) | copy-start | bytes 40
  115.1 47.9 %copy-start.69 = (f32[768]{0:T(1024)}, f32[768]{0:T(1024)S(1)}, u32[]{:S(2)}) copy-start(f32[768]{0:T(1024)S(1)} %get-tuple-element.139) | copy-start | bytes 9220
  123.4 146.1 %copy-start.44 = (bf16[3,768]{1,0:T(4,128)(2,1)}, bf16[3,768]{1,0:T(4,128)(2,1)S(1)}, u32[]{:S(2)}) copy-start(bf16[3,768]{1,0:T(4,128)(2,1)S(1)} %multiply_convert_fusion.6) | copy-start | bytes 13828
  127.4 32.9 %copy-start.10 = (bf16[512,768]{1,0:T(8,128)(2,1)S(1)}, bf16[512,768]{1,0:T(8,128)(2,1)}, u32[]{:S(2)}) copy-start(bf16[512,768]{1,0:T(8,128)(2,1)} %param.28) | copy-start | bytes 2359300
  338.9 52.3 %copy-start.2 = (f32[512,768]{1,0:T(8,128)}, f32[512,768]{1,0:T(8,128)S(1)}, u32[]{:S(2)}) copy-start(f32[512,768]{1,0:T(8,128)S(1)} %subtract_add_fusion) | copy-start | bytes 4718596
  339.7 51.4 %copy-start.57 = (bf16[768,2432]{1,0:T(8,128)(2,1)S(1)}, bf16[768,2432]{1,0:T(8,128)(2,1)}, u32[]{:S(2)}) copy-start(bf16[768,2432]{1,0:T(8,128)(2,1)} %all-gather.11.cloned.1.call-done) | copy-start | bytes 11206660
  400.1 115.3 %all-gather.23.cloned.1.call-start = ((), (), s32[]{:S(2)}) async-start(), calls=%async_computation.13 | async-start | bytes 1990656 | tf_op jit(solution)/shard_map/all_gather | solution.py:394
  401.5 109.1 %copy-start.67 = (f32[512]{0:T(512)}, f32[512]{0:T(512)S(1)}, u32[]{:S(2)}) copy-start(f32[512]{0:T(512)S(1)} %dynamic-slice.17) | copy-start | bytes 6148
  401.5 30.3 %copy-start.75 = (bf16[768]{0:T(1024)(128)(2,1)S(1)}, bf16[768]{0:T(1024)(128)(2,1)}, u32[]{:S(2)}) copy-start(bf16[768]{0:T(1024)(128)(2,1)} %get-tuple-element.141) | copy-start | bytes 4612
  401.8 30.2 %copy-start.39 = (bf16[3,768]{1,0:T(4,128)(2,1)S(1)}, bf16[3,768]{1,0:T(4,128)(2,1)}, u32[]{:S(2)}) copy-start(bf16[3,768]{1,0:T(4,128)(2,1)} %copy-done.38) | copy-start | bytes 13828
  401.8 30.2 %copy-start.41 = (bf16[3,768]{1,0:T(4,128)(2,1)S(1)}, bf16[3,768]{1,0:T(4,128)(2,1)}, u32[]{:S(2)}) copy-start(bf16[3,768]{1,0:T(4,128)(2,1)} %copy-done.40) | copy-start | bytes 13828
  401.8 30.2 %copy-start.43 = (bf16[3,768]{1,0:T(4,128)(2,1)S(1)}, bf16[3,768]{1,0:T(4,128)(2,1)}, u32[]{:S(2)}) copy-start(bf16[3,768]{1,0:T(4,128)(2,1)} %copy-done.42) | copy-start | bytes 13828
  401.8 30.2 %copy-start.45 = (bf16[3,768]{1,0:T(4,128)(2,1)S(1)}, bf16[3,768]{1,0:T(4,128)(2,1)}, u32[]{:S(2)}) copy-start(bf16[3,768]{1,0:T(4,128)(2,1)} %copy-done.44) | copy-start | bytes 13828
  401.8 30.2 %copy-start.47 = (bf16[3,768]{1,0:T(4,128)(2,1)S(1)}, bf16[3,768]{1,0:T(4,128)(2,1)}, u32[]{:S(2)}) copy-start(bf16[3,768]{1,0:T(4,128)(2,1)} %copy-done.46) | copy-start | bytes 13828
  401.8 30.2 %copy-start.49 = (bf16[3,768]{1,0:T(4,128)(2,1)S(1)}, bf16[3,768]{1,0:T(4,128)(2,1)}, u32[]{:S(2)}) copy-start(bf16[3,768]{1,0:T(4,128)(2,1)} %param.51) | copy-start | bytes 13828
  401.8 30.2 %copy-start.51 = (bf16[3,768]{1,0:T(4,128)(2,1)S(1)}, bf16[3,768]{1,0:T(4,128)(2,1)}, u32[]{:S(2)}) copy-start(bf16[3,768]{1,0:T(4,128)(2,1)} %copy-done.50) | copy-start | bytes 13828
  433.9 133.8 %reduce-scatter.13.cloned.1.call-start = ((), (), s32[]{:S(2)}) async-start(), calls=%async_computation.14 | async-start | bytes 5529600
  448.1 30.9 %copy-start.59 = (f32[768]{0:T(1024)S(1)}, f32[768]{0:T(1024)}, u32[]{:S(2)}) copy-start(f32[768]{0:T(1024)} %copy-done.58) | copy-start | bytes 9220
  491.6 133.7 %reduce-scatter.9.cloned.1.call-start = ((), (), s32[]{:S(2)}) async-start(), calls=%async_computation.11 | async-start | bytes 5308416 | tf_op jit(solution)/shard_map/reduce_scatter | solution.py:421
  499.6 183.1 %reduce-scatter.11.cloned.1.call-start = ((), (), s32[]{:S(2)}) async-start(), calls=%async_computation.12 | async-start | bytes 5308416 | tf_op jit(solution)/shard_map/reduce_scatter | solution.py:421
  509.4 260.3 %all-reduce.8.cloned.1.call-start = ((), (), s32[]{:S(2)}) async-start(), calls=%async_computation.15 | async-start | bytes 3997696 | tf_op jit(solution)/shard_map/psum | solution.py:420
  537.9 148.6 %copy-start.14 = (bf16[288,768]{1,0:T(8,128)(2,1)S(1)}, bf16[288,768]{1,0:T(8,128)(2,1)}, u32[]{:S(2)}) copy-start(bf16[288,768]{1,0:T(8,128)(2,1)} %select_n.124) | copy-start | bytes 1327108
  538.0 150.4 %copy-start.15 = (bf16[288,768]{1,0:T(8,128)(2,1)S(1)}, bf16[288,768]{1,0:T(8,128)(2,1)}, u32[]{:S(2)}) copy-start(bf16[288,768]{1,0:T(8,128)(2,1)} %select_n.126) | copy-start | bytes 1327108
  540.0 150.4 %copy-start.27 = (bf16[24,768]{1,0:T(8,128)(2,1)S(1)}, bf16[24,768]{1,0:T(8,128)(2,1)}, u32[]{:S(2)}) copy-start(bf16[24,768]{1,0:T(8,128)(2,1)} %reshape.521) | copy-start | bytes 110596
  540.0 150.4 %copy-start.28 = (bf16[24,768]{1,0:T(8,128)(2,1)S(1)}, bf16[24,768]{1,0:T(8,128)(2,1)}, u32[]{:S(2)}) copy-start(bf16[24,768]{1,0:T(8,128)(2,1)} %reshape.520) | copy-start | bytes 110596
  540.0 150.4 %copy-start.29 = (bf16[24,768]{1,0:T(8,128)(2,1)S(1)}, bf16[24,768]{1,0:T(8,128)(2,1)}, u32[]{:S(2)}) copy-start(bf16[24,768]{1,0:T(8,128)(2,1)} %reshape.518) | copy-start | bytes 110596
  570.0 121.8 %copy-start.85 = (f32[512]{0:T(512)S(1)}, f32[512]{0:T(512)}, u32[]{:S(2)}) copy-start(f32[512]{0:T(512)} %get-tuple-element.133) | copy-start | bytes 6148
  570.0 121.8 %copy-start.4 = (f32[512,768]{1,0:T(8,128)S(1)}, f32[512,768]{1,0:T(8,128)}, u32[]{:S(2)}) copy-start(f32[512,768]{1,0:T(8,128)} %copy-done.2) | copy-start | bytes 4718596
  570.0 121.8 %copy-start.11 = (bf16[512,768]{1,0:T(8,128)(2,1)S(1)}, bf16[512,768]{1,0:T(8,128)(2,1)}, u32[]{:S(2)}) copy-start(bf16[512,768]{1,0:T(8,128)(2,1)} %param.28) | copy-start | bytes 2359300
  570.0 121.8 %copy-start.53 = (f32[3,768]{1,0:T(4,128)S(1)}, f32[3,768]{1,0:T(4,128)}, u32[]{:S(2)}) copy-start(f32[3,768]{1,0:T(4,128)} %get-tuple-element.224) | copy-start | bytes 27652
  570.0 121.8 %copy-start.54 = (f32[3,768]{1,0:T(4,128)S(1)}, f32[3,768]{1,0:T(4,128)}, u32[]{:S(2)}) copy-start(f32[3,768]{1,0:T(4,128)} %get-tuple-element.151) | copy-start | bytes 27652
  570.1 121.8 %copy-start.60 = (f32[768]{0:T(1024)S(1)}, f32[768]{0:T(1024)}, u32[]{:S(2)}) copy-start(f32[768]{0:T(1024)} %copy-done.58) | copy-start | bytes 9220
  570.1 121.8 %copy-start.68 = (f32[512]{0:T(512)S(1)}, f32[512]{0:T(512)}, u32[]{:S(2)}) copy-start(f32[512]{0:T(512)} %copy-done.67) | copy-start | bytes 6148
  570.1 121.8 %copy-start.74 = (f32[512,1]{0,1:T(1,128)S(1)}, f32[512,1]{0,1:T(1,128)}, u32[]{:S(2)}) copy-start(f32[512,1]{0,1:T(1,128)} %multiply_multiply_fusion.2) | copy-start | bytes 6148
  570.1 121.8 %copy-start.80 = (f32[3]{0:T(128)S(1)}, f32[3]{0:T(128)}, u32[]{:S(2)}) copy-start(f32[3]{0:T(128)} %copy-done.78) | copy-start | bytes 40
  570.1 121.8 %copy-start.87 = (f32[3]{0:T(128)S(1)}, f32[3]{0:T(128)}, u32[]{:S(2)}) copy-start(f32[3]{0:T(128)} %get-tuple-element.196) | copy-start | bytes 40
  570.1 121.8 %copy-start.89 = (f32[3]{0:T(128)S(1)}, f32[3]{0:T(128)}, u32[]{:S(2)}) copy-start(f32[3]{0:T(128)} %broadcast_multiply_fusion.2) | copy-start | bytes 40
  (59 other events, 500.4 us)
Sparse Core Ops, SparseCore 0:
  9.7 66.1 all-gather.12
  78.4 33.4 all-gather.10
  114.3 43.8 all-gather.14
  160.0 38.9 all-gather.16
  200.6 68.7 all-gather.18
  271.2 38.9 all-gather.20
  400.2 78.7 reduce-scatter.6
  481.5 27.8 all-gather.22
  512.8 54.8 reduce-scatter.12
  571.4 53.8 reduce-scatter.8
  628.8 53.8 reduce-scatter.10
  685.9 83.7 all-reduce.7
